TPU v7x, 256 devices: a whole 4x4x8 slice. The times are simulated.
256 devices in a mesh: row: 8 (over z_lo, core), col: 32 (over z_hi, y, x).
Axes of the slice: x: 4, y: 4, z: 8 (z_hi: 2, z_lo: 4; z = z_hi * 4 + z_lo), core: 2. Of those that a mesh axis runs over, the one named last changes fastest.
Arguments:
- features: bfloat16 [65536, 512], P(('row', 'col')), may hold values from -6 to 6
- pre_act: bfloat16 [65536, 512], P(('row', 'col')), may hold values from -6 to 6
- out_grad: bfloat16 [65536, 512], P(('row', 'col')), may hold values from -6 to 6
- weight: bfloat16 [512, 512], replicated, may hold values from -0.25 to 0.25
- tile_rows: int32 [8, 32, 256], P('row', 'col'), may hold values from 0 to 63
- tile_cols: int32 [8, 32, 256], P('row', 'col'), may hold values from 0 to 15
- tile_vals: bfloat16 [8, 32, 256, 128, 128], P('row', 'col'), may hold values from -0.0625 to 0.0625
- tile_counts: int32 [8, 32], P('row', 'col'), may hold values from 32 to 256, as said below
Outputs:
- feat_grad: bfloat16 [65536, 512], P(('row', 'col'))
- weight_grad: float32 [512, 512], replicated
- bias_grad: float32 [512], replicated
Inputs may be any that keep to these rules, and one draw needn't show every extreme that they name: `tile_counts`: each grid cell holds 256, 128, 64 or 32 live tiles; at least one cell holds 256.
All inputs are finite; a program needn't handle non-finite values.
Results may differ from a plain program's by a relative error of at most 0.0049.
Values may be sent and summed in bfloat16 or wider, within the bound.
A program may use at most 128 MiB of HBM per device.

v0:
```python
import math

import jax
import jax.numpy as jnp
from jax import lax
from jax.sharding import PartitionSpec as P


def local(features, pre_act, out_grad, weight, tile_rows, tile_cols, tile_vals, tile_counts):
    width = features.shape[1]
    masked = jnp.where(pre_act > 0, out_grad, jnp.zeros_like(out_grad))
    grad_panel = lax.all_gather(masked, "col", axis=0, tiled=True)
    grad_blocks = grad_panel.reshape(-1, 128, width)
    col_blocks = features.shape[0] * lax.axis_size("row") // 128
    slots = tile_rows.shape[2]
    tile_group = math.gcd(slots, 64)
    block_rows = tile_rows.reshape(slots)
    block_cols = tile_cols.reshape(slots)
    values = tile_vals.reshape(slots, 128, 128)
    live_count = tile_counts.reshape(())

    def add_tiles(column_acc, group_index):
        first_tile = group_index * tile_group
        rows_now = lax.dynamic_slice_in_dim(block_rows, first_tile, tile_group, 0)
        cols_now = lax.dynamic_slice_in_dim(block_cols, first_tile, tile_group, 0)
        vals_now = lax.dynamic_slice_in_dim(values, first_tile, tile_group, 0)
        gathered = jnp.take(grad_blocks, rows_now, axis=0)
        products = jnp.einsum(
            "kab,kaf->kbf", vals_now, gathered, preferred_element_type=jnp.float32
        )
        active = first_tile + jnp.arange(tile_group, dtype=jnp.int32) < live_count
        products = jnp.where(active[:, None, None], products, jnp.zeros_like(products))
        column_acc = column_acc + jax.ops.segment_sum(products, cols_now, num_segments=col_blocks)
        return (column_acc, None)

    start_acc = jnp.zeros((col_blocks, 128, width), jnp.float32)
    partial_sum = lax.scan(add_tiles, start_acc, jnp.arange(slots // tile_group, dtype=jnp.int32))[
        0
    ]
    partial_sum = partial_sum.reshape(-1, width)
    summed = lax.psum_scatter(partial_sum, "row", scatter_dimension=0, tiled=True)
    feat_grad = jnp.dot(
        summed.astype(jnp.bfloat16), weight.T, preferred_element_type=jnp.float32
    ).astype(jnp.bfloat16)
    contract = (((0,), (0,)), ((), ()))
    local_weight = lax.dot_general(
        features.astype(jnp.float32), summed, contract, precision=lax.Precision.HIGHEST
    )
    local_bias = jnp.sum(masked.astype(jnp.float32), axis=0)
    weight_total, bias_total = lax.psum((local_weight, local_bias), ("row", "col"))
    vertices = features.shape[0] * lax.axis_size("row") * lax.axis_size("col")
    norm_scale = 1.0 / math.sqrt(vertices)
    return (feat_grad, weight_total * norm_scale, bias_total * norm_scale)


def solution(mesh):
    placed = (
        P(("row", "col"), None),
        P(("row", "col"), None),
        P(("row", "col"), None),
        P(),
        P("row", "col", None),
        P("row", "col", None),
        P("row", "col", None, None, None),
        P("row", "col"),
    )
    return jax.shard_map(
        local,
        mesh=mesh,
        in_specs=placed,
        out_specs=(P(("row", "col"), None), P(), P()),
        check_vma=False,
    )
```

profile of v0, /device:TPU:1, one launch (start us, length us, event | category | flops | bytes accessed | tf_op | source)
XLA Modules:
  0.0 728.6 jit_solution(8640299591339010305)
XLA Ops:
  7.2 0.0 copy-start
  7.2 0.0 all-gather.2.cloned.1.call-start
  7.2 1.9 convert_reduce_fusion
  9.1 0.0 all-gather.2.cloned.1.call-update
  9.1 0.0 copy-start.2
  9.1 0.0 copy-start.3
  9.2 0.0 reduce-scatter.2.cloned.1.call-start
  9.2 11.9 %copy.11 = bf16[1,1,256,128,128]{3,4,2,1,0:T(8,128)(2,1)} copy(bf16[1,1,256,128,128]{4,3,2,1,0:T(8,128)(2,1)} %param.16) | data formatting | bytes 16777216 | tf_op args[6]
  21.1 145.3 %all-gather.2.cloned.1.call-done = bf16[8192,512]{1,0:T(8,128)(2,1)} async-done(((bf16[256,512]{1,0:T(8,128)(2,1)}), bf16[8192,512]{1,0:T(8,128)(2,1)}) %all-gather.2.cloned.1.call-update) | async-done | bytes 8388624 | tf_op jit(solution)/shard_map/all_gather | solution.py:12
  166.4 2.4 broadcast.21
  168.9 0.0 copy-done.2
  168.9 0.0 copy-done.3
  168.9 0.0 copy-start.1
  168.9 237.0 %while.10 = (s32[]{:T(128)}, f32[16,128,512]{2,1,0:T(8,128)}, s32[4]{0:T(128)S(1)}, s32[256]{0:T(256)S(1)}, s32[]{:T(128)}, /*index=5*/bf16[256,128,128]{1,2,0:T...) while((s32[]{:T(128)}, f32[16,128,512]{2,1,0:T(8,128)}, ...), condition=%wide.region_2.3_spmd, body=%wide.region_0.2_spmd.sunk | while | flops 1086326272 | bytes 94378176 | solution.py:37
  168.9 0.6 dynamic_slice.21
  170.1 0.7 compare_and_fusion.2
  170.9 8.9 %gather_fusion = bf16[64,128,512]{2,1,0:T(8,128)(2,1)} fusion(bf16[64,128,512]{2,1,0:T(8,128)(2,1)} %get-tuple-element.156, s32[1024]{0:T(1024)S(1)} %pad_clamp_fusion.2), kind=kCustom, calls=%fused_computation.clone.1 | custom fusion | bytes 16777472 | tf_op jit(solution)/shard_map/while/body/eval_jaxpr/jit(_take)/gather | solution.py:27
  179.8 12.1 %convolution_select_fusion.2 = f32[64,128,512]{2,1,0:T(8,128)} fusion(bf16[64,128,512]{2,1,0:T(8,128)(2,1)} %gather_fusion, pred[64]{0:T(512)(128)(4,1)S(1)} %get-tuple-element.123, pred[64]{0:T(512)(128)(4,1)S(1)} %get-tuple-element.124, bf16[256,128,128]{1,2,0:T(8,128)(2,1)} %get-tuple-element.154, s32[]{:T(128)S(6)} %select_n.35), kind=kOutput, calls=%fused_computation.2.clone.1 | convolution fusion | flops 1082130432 | bytes 27263108 | tf_op jit(solution)/shard_map/while/body/eval_jaxpr/kab,kaf->kbf/dot_general | solution.py:28
  191.9 0.1 dynamic_slice.22
  192.0 36.3 %scatter_fusion = f32[16,128,512]{2,1,0:T(8,128)} fusion(f32[16,128,512]{2,1,0:T(8,128)} %get-tuple-element.138, s32[64]{0:T(128)S(1)} %dynamic_slice.22, f32[64,128,512]{2,1,0:T(8,128)} %convolution_select_fusion.2), kind=kCustom, calls=%fused_computation.1.clone.1 | custom fusion | flops 4194304 | bytes 50331904 | tf_op jit(solution)/shard_map/while/body/eval_jaxpr/scatter-add | solution.py:33
  228.3 0.6 dynamic_slice.21
  229.5 0.7 compare_and_fusion.2
  230.2 8.9 %gather_fusion = bf16[64,128,512]{2,1,0:T(8,128)(2,1)} fusion(bf16[64,128,512]{2,1,0:T(8,128)(2,1)} %get-tuple-element.156, s32[1024]{0:T(1024)S(1)} %pad_clamp_fusion.2), kind=kCustom, calls=%fused_computation.clone.1 | custom fusion | bytes 16777472 | tf_op jit(solution)/shard_map/while/body/eval_jaxpr/jit(_take)/gather | solution.py:27
  239.1 12.1 %convolution_select_fusion.2 = f32[64,128,512]{2,1,0:T(8,128)} fusion(bf16[64,128,512]{2,1,0:T(8,128)(2,1)} %gather_fusion, pred[64]{0:T(512)(128)(4,1)S(1)} %get-tuple-element.123, pred[64]{0:T(512)(128)(4,1)S(1)} %get-tuple-element.124, bf16[256,128,128]{1,2,0:T(8,128)(2,1)} %get-tuple-element.154, s32[]{:T(128)S(6)} %select_n.35), kind=kOutput, calls=%fused_computation.2.clone.1 | convolution fusion | flops 1082130432 | bytes 27263108 | tf_op jit(solution)/shard_map/while/body/eval_jaxpr/kab,kaf->kbf/dot_general | solution.py:28
  251.3 0.1 dynamic_slice.22
  251.4 36.1 %scatter_fusion = f32[16,128,512]{2,1,0:T(8,128)} fusion(f32[16,128,512]{2,1,0:T(8,128)} %get-tuple-element.138, s32[64]{0:T(128)S(1)} %dynamic_slice.22, f32[64,128,512]{2,1,0:T(8,128)} %convolution_select_fusion.2), kind=kCustom, calls=%fused_computation.1.clone.1 | custom fusion | flops 4194304 | bytes 50331904 | tf_op jit(solution)/shard_map/while/body/eval_jaxpr/scatter-add | solution.py:33
  287.5 0.6 dynamic_slice.21
  288.7 0.7 compare_and_fusion.2
  289.4 8.9 %gather_fusion = bf16[64,128,512]{2,1,0:T(8,128)(2,1)} fusion(bf16[64,128,512]{2,1,0:T(8,128)(2,1)} %get-tuple-element.156, s32[1024]{0:T(1024)S(1)} %pad_clamp_fusion.2), kind=kCustom, calls=%fused_computation.clone.1 | custom fusion | bytes 16777472 | tf_op jit(solution)/shard_map/while/body/eval_jaxpr/jit(_take)/gather | solution.py:27
  298.3 12.1 %convolution_select_fusion.2 = f32[64,128,512]{2,1,0:T(8,128)} fusion(bf16[64,128,512]{2,1,0:T(8,128)(2,1)} %gather_fusion, pred[64]{0:T(512)(128)(4,1)S(1)} %get-tuple-element.123, pred[64]{0:T(512)(128)(4,1)S(1)} %get-tuple-element.124, bf16[256,128,128]{1,2,0:T(8,128)(2,1)} %get-tuple-element.154, s32[]{:T(128)S(6)} %select_n.35), kind=kOutput, calls=%fused_computation.2.clone.1 | convolution fusion | flops 1082130432 | bytes 27263108 | tf_op jit(solution)/shard_map/while/body/eval_jaxpr/kab,kaf->kbf/dot_general | solution.py:28
  310.5 0.1 dynamic_slice.22
  310.6 36.0 %scatter_fusion = f32[16,128,512]{2,1,0:T(8,128)} fusion(f32[16,128,512]{2,1,0:T(8,128)} %get-tuple-element.138, s32[64]{0:T(128)S(1)} %dynamic_slice.22, f32[64,128,512]{2,1,0:T(8,128)} %convolution_select_fusion.2), kind=kCustom, calls=%fused_computation.1.clone.1 | custom fusion | flops 4194304 | bytes 50331904 | tf_op jit(solution)/shard_map/while/body/eval_jaxpr/scatter-add | solution.py:33
  346.6 0.6 dynamic_slice.21
  347.8 0.7 compare_and_fusion.2
  348.5 8.9 %gather_fusion = bf16[64,128,512]{2,1,0:T(8,128)(2,1)} fusion(bf16[64,128,512]{2,1,0:T(8,128)(2,1)} %get-tuple-element.156, s32[1024]{0:T(1024)S(1)} %pad_clamp_fusion.2), kind=kCustom, calls=%fused_computation.clone.1 | custom fusion | bytes 16777472 | tf_op jit(solution)/shard_map/while/body/eval_jaxpr/jit(_take)/gather | solution.py:27
  357.4 12.1 %convolution_select_fusion.2 = f32[64,128,512]{2,1,0:T(8,128)} fusion(bf16[64,128,512]{2,1,0:T(8,128)(2,1)} %gather_fusion, pred[64]{0:T(512)(128)(4,1)S(1)} %get-tuple-element.123, pred[64]{0:T(512)(128)(4,1)S(1)} %get-tuple-element.124, bf16[256,128,128]{1,2,0:T(8,128)(2,1)} %get-tuple-element.154, s32[]{:T(128)S(6)} %select_n.35), kind=kOutput, calls=%fused_computation.2.clone.1 | convolution fusion | flops 1082130432 | bytes 27263108 | tf_op jit(solution)/shard_map/while/body/eval_jaxpr/kab,kaf->kbf/dot_general | solution.py:28
  369.6 0.1 dynamic_slice.22
  369.6 36.2 %scatter_fusion = f32[16,128,512]{2,1,0:T(8,128)} fusion(f32[16,128,512]{2,1,0:T(8,128)} %get-tuple-element.138, s32[64]{0:T(128)S(1)} %dynamic_slice.22, f32[64,128,512]{2,1,0:T(8,128)} %convolution_select_fusion.2), kind=kCustom, calls=%fused_computation.1.clone.1 | custom fusion | flops 4194304 | bytes 50331904 | tf_op jit(solution)/shard_map/while/body/eval_jaxpr/scatter-add | solution.py:33
  405.8 0.0 reduce-scatter.2.cloned.1.call-update
  405.9 0.0 all-reduce.2.cloned.1.call-start
  405.9 51.8 %reduce-scatter.2.cloned.1.call-done = f32[256,512]{1,0:T(8,128)} async-done(((f32[2048,512]{1,0:T(8,128)}), f32[256,512]{1,0:T(8,128)}) %reduce-scatter.2.cloned.1.call-update) | async-done | bytes 524304 | tf_op jit(solution)/shard_map/reduce_scatter | solution.py:41
  457.7 0.0 copy-done.1
  457.7 2.6 convolution_bitcast_fusion
  460.3 0.0 all-reduce.2.cloned.1.call-update
  460.3 80.3 %psum.15 = f32[512]{0:T(512)S(1)} all-reduce(f32[512]{0:T(512)S(1)} %get-tuple-element.67), channel_id=1, replica_groups=mesh['row'=8,'col'=32] {'row','col'}, use_global_device_ids=true, to_apply=%region_6.7 | all-reduce | flops 512 | bytes 4096 | tf_op jit(solution)/shard_map/psum | solution.py:50
  540.6 0.6 broadcast_multiply_fusion.1
  541.2 0.0 copy-done
  541.2 2.1 convolution_convert_fusion
  543.3 176.2 %all-reduce.2.cloned.1.call-done = f32[512,512]{0,1:T(8,128)} async-done(((f32[512,512]{0,1:T(8,128)}), f32[512,512]{0,1:T(8,128)}) %all-reduce.2.cloned.1.call-update) | async-done | bytes 1048592 | tf_op jit(solution)/shard_map/psum | solution.py:50
  719.5 1.3 broadcast_multiply_fusion
  720.8 1.3 copy.12
  (5 shorter events, 0.0 us)
Async XLA Ops:
  7.2 534.1 %copy-start = (bf16[512,512]{1,0:T(8,128)(2,1)S(1)}, bf16[512,512]{1,0:T(8,128)(2,1)}, u32[]{:S(2)}) copy-start(bf16[512,512]{1,0:T(8,128)(2,1)} %param.13) | copy-start | bytes 1572868
  7.2 159.2 %all-gather.2.cloned.1.call-start = ((), (), s32[]{:S(2)}) async-start(), calls=%async_computation.1 | async-start | bytes 8650752 | tf_op jit(solution)/shard_map/all_gather | solution.py:12
  9.1 159.7 %copy-start.2 = (s32[1,1,256]{2,1,0:T(1,128)S(1)}, s32[1,1,256]{2,1,0:T(1,128)}, u32[]{:S(2)}) copy-start(s32[1,1,256]{2,1,0:T(1,128)} %param.14) | copy-start | bytes 3076
  9.1 159.7 %copy-start.3 = (s32[1,1,256]{2,1,0:T(1,128)S(1)}, s32[1,1,256]{2,1,0:T(1,128)}, u32[]{:S(2)}) copy-start(s32[1,1,256]{2,1,0:T(1,128)} %param.15) | copy-start | bytes 3076
  9.2 448.5 %reduce-scatter.2.cloned.1.call-start = ((), (), s32[]{:S(2)}) async-start(), calls=%async_computation.2 | async-start | bytes 4718592 | tf_op jit(solution)/shard_map/reduce_scatter | solution.py:41
  168.9 288.8 %copy-start.1 = (bf16[256,512]{1,0:T(8,128)(2,1)S(1)}, bf16[256,512]{1,0:T(8,128)(2,1)}, u32[]{:S(2)}) copy-start(bf16[256,512]{1,0:T(8,128)(2,1)} %param.10) | copy-start | bytes 786436
  405.9 313.6 %all-reduce.2.cloned.1.call-start = ((), (), s32[]{:S(2)}) async-start(), calls=%async_computation.3 | async-start | bytes 2097152 | tf_op jit(solution)/shard_map/psum | solution.py:50
Sparse Core Ops, SparseCore 0:
  12.1 154.2 all-gather.1
  406.0 51.6 reduce-scatter.1
  463.7 255.7 all-reduce.1
where the time goes:
time: 730 us; the launch traced here: 729 us
  waiting for transfers between devices  373 us (51%)
  other arithmetic  151 us (21%)
  blocking collectives  80.3 us (11%)
  local copies, waits for them, and re-layouts  53.9 us (7%)
  matrix products  53.3 us (7%)
  between operations  13.8 us (2%)
    psum x1, waiting for transfers between devices, local(): lax.psum((local_weight, local_bias), ('row', 'col'))  176 us
    all_gather x1, waiting for transfers between devices, local(): grad_panel = lax.all_gather(masked, 'col', axis=0, tiled=True)  145 us
    scatter-add x4, other arithmetic, add_tiles(): jax.ops.segment_sum(products, cols_now, num_segments=col_blocks)  145 us
    psum x1, blocking collectives, local(): lax.psum((local_weight, local_bias), ('row', 'col'))  80.3 us
    reduce_scatter x1, waiting for transfers between devices, local(): lax.psum_scatter(partial_sum, 'row', scatter_dimension=0, tiled=True)  51.8 us
    dot_general x4, matrix products, add_tiles(): jnp.einsum('kab,kaf->kbf', vals_now, gathered, preferred_element_type=jnp...  48.6 us
    gather x4, local copies, waits for them, and re-layouts, add_tiles(): gathered = jnp.take(grad_blocks, rows_now, axis=0)  35.6 us
  transfers between devices with their start and end apart: 3, of which 3 were waited for; matrix products, arithmetic and copies ran while one was open for 2% of the time, Pallas kernels for 0%

commit v1 on v0

v1 whole, which is shorter than its diff:
```python
import functools
import math

import jax
import jax.numpy as jnp
from jax import lax
from jax.experimental import pallas as pl
from jax.experimental.pallas import tpu as pltpu
from jax.sharding import PartitionSpec as P

AG_CHUNKS = 2
CHUNKS = 4
BLOCK = 128
MESH = pl.DeviceIdType.MESH


def gather_body(
    pre, cot, panel, bias_out, own_blocks, ag_send, ag_recv, own_sem
):
    rows_dev, width = pre.shape
    chunk = width // AG_CHUNKS
    half_chunk = chunk // 2

    r = lax.axis_index("row")
    c = lax.axis_index("col")
    zl, core = r // 2, r % 2
    zh, m = c // 16, c % 16
    y, x = m // 4, m % 4
    w8 = zh * 4 + zl
    partner = (r + 1 - 2 * core, c)
    z_partner = (r, (1 - zh) * 16 + m)

    def plane_peer(d):
        return (r, zh * 16 + (m + d) % 16)

    def z_peer(d):
        q = (w8 + d) % 8
        return (2 * (q % 4) + core, (q // 4) * 16 + m)

    def neighbour(dim, d):
        if dim == 0:
            return (r, zh * 16 + y * 4 + (x + d) % 4)
        return (r, zh * 16 + ((y + d) % 4) * 4 + x)

    def remote(src, dst, send_sem, recv_sem, device):
        return pltpu.make_async_remote_copy(
            src_ref=src, dst_ref=dst, send_sem=send_sem, recv_sem=recv_sem,
            device_id=device, device_id_type=MESH,
        )

    def wait_recv(ref, send_sem, recv_sem):
        remote(ref, ref, send_sem, recv_sem, partner).wait_recv()

    def wait_send(ref, send_sem, recv_sem):
        remote(ref, ref, send_sem, recv_sem, partner).wait_send()

    barrier = pltpu.get_barrier_semaphore()
    for device in (
        z_partner, neighbour(0, 1), neighbour(0, -1), neighbour(1, 1), neighbour(1, -1)
    ):
        pl.semaphore_signal(barrier, inc=1, device_id=device, device_id_type=MESH)

    def block_of(plane, d1, d2, h):
        if h == 0:
            xx, yy = (x + d1) % 4, (y + d2) % 4
        else:
            xx, yy = (x + d2) % 4, (y + d1) % 4
        return 2 * (plane * 16 + yy * 4 + xx) + h

    def ag_copy(k, b, device, part=None, h=None):
        ref = panel.at[k, b]
        if part is not None:
            ref = panel.at[k, b, pl.ds(part * half_chunk, half_chunk)]
        src = ref if h is None else own_blocks.at[k, h]
        remote(src, ref, ag_send.at[k], ag_recv.at[k, b], device).start()

    def ag_wait(k, b):
        wait_recv(panel.at[k, b], ag_send.at[k], ag_recv.at[k, b])

    def first_dim(h):
        return 0 if h == 0 else 1

    def second_dim(h):
        return 1 if h == 0 else 0

    def s0(k, plane, mine):
        for dim in (first_dim, second_dim):
            for h in (0, 1):
                b = block_of(plane, 0, 0, h)
                for d in (1, -1):
                    ag_copy(k, b, neighbour(dim(h), d), None, h if mine else None)

    def s1(k, plane):
        for d in (-1, 1):
            for h in (0, 1):
                b = block_of(plane, d, 0, h)
                ag_wait(k, b)
                ag_copy(k, b, neighbour(first_dim(h), -d), 0 if d == -1 else 1)
                for e in (1, -1):
                    ag_copy(k, b, neighbour(second_dim(h), e))

    def s2(k, plane):
        for h in (0, 1):
            b = block_of(plane, 2, 0, h)
            ag_wait(k, b)
            for e in (1, -1):
                ag_copy(k, b, neighbour(second_dim(h), e))

    def s3(k, plane):
        for d1 in (0, -1, 1, 2):
            for d in (-1, 1):
                for h in (0, 1):
                    b = block_of(plane, d1, d, h)
                    ag_wait(k, b)
                    ag_copy(k, b, neighbour(second_dim(h), -d), 0 if d == -1 else 1)

    def s4(k, plane):
        for d1 in (0, -1, 1, 2):
            for h in (0, 1):
                ag_wait(k, block_of(plane, d1, 2, h))

    def z_go(k):
        for h in (0, 1):
            b = block_of(zh, 0, 0, h)
            ag_copy(k, b, z_partner, None, h)

    def z_come(k):
        for h in (0, 1):
            ag_wait(k, block_of(1 - zh, 0, 0, h))
        s0(k, 1 - zh, False)

    places = []

    def prepare(k):
        lanes = pl.ds(k * chunk, chunk)
        kept = jnp.where(
            pre[:, lanes].astype(jnp.float32) > 0, cot[:, lanes].astype(jnp.float32), 0.0
        )
        for h in (0, 1):
            part = kept[h * BLOCK:(h + 1) * BLOCK, :]
            own_blocks[k, h] = part.T.astype(jnp.bfloat16)
        place = pltpu.make_async_copy(
            own_blocks.at[k], panel.at[k, pl.ds(2 * c, 2)], own_sem.at[k]
        )
        place.start()
        places.append(place)
        return jnp.sum(kept, axis=0, keepdims=True)

    bias_rows = [prepare(0)]
    pl.semaphore_wait(barrier, 5)
    s0(0, zh, True)
    z_go(0)
    for k in range(1, AG_CHUNKS):
        bias_rows.append(prepare(k))
        s0(k, zh, True)
        z_go(k)
    bias_out[...] = jnp.concatenate(bias_rows, axis=1)
    for k in range(AG_CHUNKS):
        s1(k, zh)
        s2(k, zh)
        if k > 0:
            s3(k - 1, 1 - zh)
            s4(k - 1, zh)
            s4(k - 1, 1 - zh)
        z_come(k)
        s3(k, zh)
        s1(k, 1 - zh)
        s2(k, 1 - zh)
    k = AG_CHUNKS - 1
    s3(k, 1 - zh)
    s4(k, zh)
    s4(k, 1 - zh)
    for place in places:
        place.wait()
    for k in range(AG_CHUNKS):
        wait_send(panel.at[k, pl.ds(0, 62)], ag_send.at[k], ag_recv.at[k, 0])


def order_body(trow, tcol, count, meta_v):
    n_tiles = trow.shape[1]
    n_cols = 16
    lane = lax.broadcasted_iota(jnp.int32, (n_tiles, n_tiles), 1)
    sub = lax.broadcasted_iota(jnp.int32, (n_tiles, n_tiles), 0)
    live = count[0, 0]
    lane1 = lax.broadcasted_iota(jnp.int32, (1, n_tiles), 1)
    col_r = jnp.where(lane1 < live, tcol[...], 100)
    diag = lane == sub
    col_c = jnp.sum(jnp.where(diag, col_r, 0), axis=1, keepdims=True)
    row_c = jnp.sum(jnp.where(diag, trow[...], 0), axis=1, keepdims=True)
    rank_c = jnp.sum(
        jnp.where((col_r == col_c) & (lane < sub), 1, 0), axis=1, keepdims=True
    )
    lane_j = lax.broadcasted_iota(jnp.int32, (n_tiles, BLOCK), 1)
    n_r = jnp.sum(jnp.where(col_c == lane_j, 1, 0), axis=0, keepdims=True)
    lane_j1 = lax.broadcasted_iota(jnp.int32, (1, BLOCK), 1)
    pad_r = jnp.where(lane_j1 < n_cols, n_r + (n_r & 1), 0)
    base_c = jnp.sum(jnp.where(lane_j < col_c, pad_r, 0), axis=1, keepdims=True)
    pos_c = jnp.where(col_c < n_cols, base_c + rank_c, 100000)
    jj_lane = lax.broadcasted_iota(jnp.int32, (BLOCK, BLOCK), 1)
    jj_sub = lax.broadcasted_iota(jnp.int32, (BLOCK, BLOCK), 0)
    pad_c = jnp.sum(jnp.where(jj_lane == jj_sub, pad_r, 0), axis=1, keepdims=True)
    end_r = jnp.sum(jnp.where(jj_sub <= jj_lane, pad_c, 0), axis=0, keepdims=True)
    last_r = jnp.maximum(end_r // 2 - 1, 0)
    has_r = jnp.where(n_r > 0, 1, 0)
    meta_w = meta_v.shape[1]
    lane_p = lax.broadcasted_iota(jnp.int32, (n_tiles, meta_w), 1)
    sub_p = lax.broadcasted_iota(jnp.int32, (n_tiles, meta_w), 0)
    hit = lane_p == pos_c
    meta_v[...] = jnp.zeros(meta_v.shape, jnp.int32)
    meta_v[0:1, :] = n_tiles + jnp.sum(
        jnp.where(hit, sub_p - n_tiles, 0), axis=0, keepdims=True
    )
    meta_v[1:2, :] = jnp.sum(jnp.where(hit, row_c, 0), axis=0, keepdims=True)
    meta_v[2:3, :] = 1 - jnp.sum(jnp.where(hit & (rank_c == 0), 1, 0), axis=0, keepdims=True)
    meta_v[3:4, 0:BLOCK] = last_r
    meta_v[4:5, 0:BLOCK] = has_r
    meta_v[5:6, 0:BLOCK] = jnp.sum(pad_r, axis=1, keepdims=True) // 2 + 0 * lane_j1


def product_body(meta_s, panel, vals, own, send, slots):
    chunk = panel.shape[1]
    core = lax.axis_index("row") % 2
    pairs = meta_s[5, 0]

    def step(p, acc):
        lhs = jnp.concatenate(
            [panel[meta_s[1, 2 * p]], panel[meta_s[1, 2 * p + 1]]], axis=1
        )
        both = [
            vals[jnp.minimum(meta_s[0, 2 * p + i], vals.shape[0] - 1)] for i in (0, 1)
        ]
        alive = (meta_s[0, 2 * p + 1] < vals.shape[0]).astype(jnp.int32).astype(jnp.bfloat16)
        rhs = jnp.concatenate([both[0], both[1] * alive], axis=0)
        keep = meta_s[2, 2 * p].astype(jnp.float32)
        acc = acc * keep + jnp.dot(lhs, rhs, preferred_element_type=jnp.float32)
        slots[p] = acc
        return acc

    def several(g, acc):
        for i in range(8):
            acc = step(8 * g + i, acc)
        return acc

    lax.fori_loop(0, (pairs + 7) // 8, several, jnp.zeros((chunk, BLOCK), jnp.float32))

    def column(j):
        return slots[meta_s[3, j]] * meta_s[4, j].astype(jnp.float32)

    for q in range(4):
        for h in (0, 1):
            other = column(2 * (2 * q + 1 - core) + h).astype(jnp.bfloat16)
            mine = column(2 * (2 * q + core) + h)
            for i in range(own.shape[0]):
                part = slice(i * own.shape[3], (i + 1) * own.shape[3])
                send[i, q, h] = other[part]
                own[i, q, h] = mine[part]


def reduce_body(
    norm_scale,
    own, send1, feat, weight, bias_in,
    fg_out, wg_out, bias_out,
    feat_t, recv1, total_f, send2, recv2, fg_acc, ar, recv_p, xs, recv_xy, zbuf, gathered, bxy, bz, bp,
    rs_send1, rs_recv1, rs_send2, rs_recv2,
    p_send, p_recv, xy_send, xy_recv, zr_send, zr_recv, g_send, g_recv, gp_send, gp_recv,
    b_send, b_recv,
):
    rows_dev, width = feat.shape
    chunk = width // CHUNKS

    r = lax.axis_index("row")
    c = lax.axis_index("col")
    zl, core = r // 2, r % 2
    zh, m = c // 16, c % 16
    y, x = m // 4, m % 4
    w8 = zh * 4 + zl
    partner = (r + 1 - 2 * core, c)
    z_partner = (r, (1 - zh) * 16 + m)

    def plane_peer(d):
        return (r, zh * 16 + (m + d) % 16)

    def z_peer(d):
        q = (w8 + d) % 8
        return (2 * (q % 4) + core, (q // 4) * 16 + m)

    def neighbour(dim, d):
        if dim == 0:
            return (r, zh * 16 + y * 4 + (x + d) % 4)
        return (r, zh * 16 + ((y + d) % 4) * 4 + x)

    def remote(src, dst, send_sem, recv_sem, device):
        return pltpu.make_async_remote_copy(
            src_ref=src, dst_ref=dst, send_sem=send_sem, recv_sem=recv_sem,
            device_id=device, device_id_type=MESH,
        )

    def wait_recv(ref, send_sem, recv_sem):
        remote(ref, ref, send_sem, recv_sem, partner).wait_recv()

    def wait_send(ref, send_sem, recv_sem):
        remote(ref, ref, send_sem, recv_sem, partner).wait_send()

    barrier = pltpu.get_barrier_semaphore()

    def greet(device):
        pl.semaphore_signal(barrier, inc=1, device_id=device, device_id_type=MESH)

    greet(partner)

    def greet_plane(d, carry):
        greet(plane_peer(d))
        return carry

    def greet_z(d, carry):
        greet(z_peer(d))
        return carry

    lax.fori_loop(1, 16, greet_plane, 0)
    lax.fori_loop(1, 8, greet_z, 0)
    bias_local = bias_in[...]
    bxy[m] = jnp.zeros(bxy.shape[1:], jnp.float32)
    for q in range(width // BLOCK):
        bxy[m, pl.ds(q, 1)] = bias_local[:, q * BLOCK:(q + 1) * BLOCK]

    def bias_plane(d, carry):
        remote(bxy.at[m], bxy.at[m], b_send.at[0], b_recv.at[0], plane_peer(d)).start()
        return carry

    def bias_z(d, carry):
        remote(bz.at[w8], bz.at[w8], b_send.at[1], b_recv.at[1], z_peer(d)).start()
        return carry

    feat_t[...] = feat[...].astype(jnp.float32).T.astype(jnp.bfloat16)
    pl.semaphore_wait(barrier, 23)
    for k in range(CHUNKS):
        remote(send1.at[k], recv1.at[k], rs_send1.at[k], rs_recv1.at[k], partner).start()

    def rs1(k):
        wait_recv(recv1.at[k], rs_send1.at[k], rs_recv1.at[k])
        for q in range(4):
            for h in (0, 1):
                total = own[k, q, h] + recv1[k, q, h].astype(jnp.float32)
                total_f[k, q, h] = total
                send2[k, q, h] = total.astype(jnp.bfloat16)
        for d in (1, 2, 3):
            q = (zl + d) % 4
            remote(
                send2.at[k, q], recv2.at[k, d - 1], rs_send2.at[k], rs_recv2.at[k],
                (2 * q + core, c),
            ).start()

    def rs2(k):
        wait_recv(recv2.at[k], rs_send2.at[k], rs_recv2.at[k])
        wg = None
        fg_parts = []
        w_part = weight[:, pl.ds(k * chunk, chunk)]
        for h in (0, 1):
            total = total_f[k, zl, h]
            for d in range(3):
                total = total + recv2[k, d, h].astype(jnp.float32)
            high = total.astype(jnp.bfloat16)
            low = (total - high.astype(jnp.float32)).astype(jnp.bfloat16)
            f_part = feat_t[:, h * BLOCK:(h + 1) * BLOCK]
            contract = (((1,), (1,)), ((), ()))
            for piece in (high, low):
                term = lax.dot_general(
                    f_part, piece, contract, preferred_element_type=jnp.float32
                )
                wg = term if wg is None else wg + term
            fg_parts.append(high)
        ar[k] = wg.reshape(ar.shape[1:])
        remote(
            ar.at[k, 1 - core], recv_p.at[k], p_send.at[k], p_recv.at[k], partner
        ).start()
        fg = jnp.dot(
            w_part, jnp.concatenate(fg_parts, axis=1), preferred_element_type=jnp.float32
        )
        if k == 0:
            fg_acc[...] = fg
        elif k < CHUNKS - 1:
            fg_acc[...] += fg
        else:
            fg_out[...] = (fg_acc[...] + fg).T.astype(jnp.bfloat16)

    def ar1(k):
        wait_recv(recv_p.at[k], p_send.at[k], p_recv.at[k])
        xs[k] = ar[k, core] + recv_p[k]

        def go(d, carry):
            remote(
                xs.at[k, (m + d) % 16], recv_xy.at[k, d - 1],
                xy_send.at[k], xy_recv.at[k], plane_peer(d),
            ).start()
            return carry

        lax.fori_loop(1, 16, go, 0)

    def ar2(k):
        wait_recv(recv_xy.at[k], xy_send.at[k], xy_recv.at[k])
        zbuf[k, w8] = xs[k, m] + jnp.sum(recv_xy[k], axis=0)

        def go(d, carry):
            remote(
                zbuf.at[k, w8], zbuf.at[k, w8], zr_send.at[k], zr_recv.at[k], z_peer(d)
            ).start()
            return carry

        lax.fori_loop(1, 8, go, 0)

    def ar3(k):
        wait_recv(zbuf.at[k, pl.ds(0, 7)], zr_send.at[k], zr_recv.at[k])
        total = zbuf[k, 0]
        for i in range(1, 8):
            total = total + zbuf[k, i]
        gathered[k, core, m] = total * norm_scale

        def go(d, carry):
            ref = gathered.at[k, core, m]
            remote(ref, ref, g_send.at[k], g_recv.at[k], plane_peer(d)).start()
            return carry

        lax.fori_loop(1, 16, go, 0)

    def ar4(k):
        wait_recv(gathered.at[k, 0, pl.ds(0, 15)], g_send.at[k], g_recv.at[k])
        ref = gathered.at[k, core]
        remote(ref, ref, gp_send.at[k], gp_recv.at[k], partner).start()

    def ar5(k):
        wait_recv(gathered.at[k, 0], gp_send.at[k], gp_recv.at[k])
        wg_out[:, pl.ds(k * chunk, chunk)] = gathered[k].reshape(width, chunk)

    def bias1():
        wait_recv(bxy.at[pl.ds(0, 15)], b_send.at[0], b_recv.at[0])
        total = bxy[0]
        for i in range(1, 16):
            total = total + bxy[i]
        bz[w8] = total
        lax.fori_loop(1, 8, bias_z, 0)

    def bias2():
        wait_recv(bz.at[pl.ds(0, 7)], b_send.at[1], b_recv.at[1])
        total = bz[0]
        for i in range(1, 8):
            total = total + bz[i]
        bp[0] = total
        remote(bp.at[0], bp.at[1], b_send.at[2], b_recv.at[2], partner).start()

    def bias3():
        wait_recv(bp.at[1], b_send.at[2], b_recv.at[2])
        bias_out[...] = (bp[0] + bp[1]) * norm_scale

    for k in range(CHUNKS):
        rs1(k)
    lax.fori_loop(1, 16, bias_plane, 0)
    bias1()
    for k in range(CHUNKS):
        rs2(k)
        if k == 0:
            bias2()
        if k >= 1:
            ar2(k - 1)
        ar1(k)
        if k >= 1:
            ar3(k - 1)
        if k >= 2:
            ar4(k - 2)
        if k >= 3:
            ar5(k - 3)
    last = CHUNKS - 1
    bias3()
    ar2(last)
    ar4(last - 1)
    ar3(last)
    ar5(last - 2)
    ar5(last - 1)
    ar4(last)
    for k in range(CHUNKS):
        wait_send(send1.at[k], rs_send1.at[k], rs_recv1.at[k])
        wait_send(send2.at[k, pl.ds(0, 3)], rs_send2.at[k], rs_recv2.at[k])
        wait_send(ar.at[k, 0], p_send.at[k], p_recv.at[k])
        wait_send(xs.at[k, pl.ds(0, 15)], xy_send.at[k], xy_recv.at[k])
        wait_send(zbuf.at[k, pl.ds(0, 7)], zr_send.at[k], zr_recv.at[k])
        wait_send(gathered.at[k, 0, pl.ds(0, 15)], g_send.at[k], g_recv.at[k])
    wait_send(bxy.at[pl.ds(0, 15)], b_send.at[0], b_recv.at[0])
    wait_send(bz.at[pl.ds(0, 7)], b_send.at[1], b_recv.at[1])
    wait_send(bp.at[0], b_send.at[2], b_recv.at[2])
    ar5(last)
    for k in range(CHUNKS):
        wait_send(gathered.at[k, 0], gp_send.at[k], gp_recv.at[k])


def local(features, pre_act, out_grad, weight, tile_rows, tile_cols, tile_vals, tile_counts):
    rows_dev, width = features.shape
    slots = tile_rows.shape[2]
    chunk = width // CHUNKS
    ag_chunk = width // AG_CHUNKS
    n_pairs = (slots + 16) // 2 + 8
    pieces = width // 32
    vertices = rows_dev * lax.axis_size("row") * lax.axis_size("col")
    bf16, f32 = jnp.bfloat16, jnp.float32
    vmem = pl.BlockSpec(memory_space=pltpu.VMEM)
    smem = pl.BlockSpec(memory_space=pltpu.SMEM)
    anywhere = pl.BlockSpec(memory_space=pl.ANY)
    dma = pltpu.SemaphoreType.DMA
    limit = 56 * 1024 * 1024
    panel, bias_rows = pl.pallas_call(
        gather_body,
        out_shape=(
            jax.ShapeDtypeStruct((AG_CHUNKS, 64, ag_chunk, BLOCK), bf16),
            jax.ShapeDtypeStruct((1, width), f32),
        ),
        in_specs=[vmem, vmem],
        out_specs=(anywhere, vmem),
        scratch_shapes=[
            pltpu.VMEM((AG_CHUNKS, 2, ag_chunk, BLOCK), bf16),
            dma((AG_CHUNKS,)), dma((AG_CHUNKS, 64)), dma((AG_CHUNKS,)),
        ],
        compiler_params=pltpu.CompilerParams(
            collective_id=0, has_side_effects=True, vmem_limit_bytes=limit
        ),
    )(pre_act, out_grad)
    meta = pl.pallas_call(
        order_body,
        out_shape=jax.ShapeDtypeStruct((8, 384), jnp.int32),
        in_specs=[vmem, vmem, smem],
        out_specs=vmem,
    )(
        tile_rows.reshape(1, slots), tile_cols.reshape(1, slots), tile_counts.reshape(1, 1)
    )
    own, send = pl.pallas_call(
        product_body,
        out_shape=(
            jax.ShapeDtypeStruct((CHUNKS, 4, 2, chunk, BLOCK), f32),
            jax.ShapeDtypeStruct((CHUNKS, 4, 2, chunk, BLOCK), bf16),
        ),
        grid_spec=pltpu.PrefetchScalarGridSpec(
            num_scalar_prefetch=1,
            grid=(AG_CHUNKS,),
            in_specs=[
                pl.BlockSpec((None, 64, ag_chunk, BLOCK), lambda k, meta: (k, 0, 0, 0)),
                pl.BlockSpec((slots, BLOCK, BLOCK), lambda k, meta: (0, 0, 0)),
            ],
            out_specs=(
                pl.BlockSpec((CHUNKS // AG_CHUNKS, 4, 2, chunk, BLOCK), lambda k, meta: (k, 0, 0, 0, 0)),
                pl.BlockSpec((CHUNKS // AG_CHUNKS, 4, 2, chunk, BLOCK), lambda k, meta: (k, 0, 0, 0, 0)),
            ),
            scratch_shapes=[pltpu.VMEM((n_pairs, ag_chunk, BLOCK), f32)],
        ),
        compiler_params=pltpu.CompilerParams(vmem_limit_bytes=limit),
    )(meta, panel, tile_vals.reshape(slots, BLOCK, BLOCK))

    fg, wg, bias = pl.pallas_call(
        functools.partial(reduce_body, 1.0 / math.sqrt(vertices)),
        out_shape=(
            jax.ShapeDtypeStruct((rows_dev, width), bf16),
            jax.ShapeDtypeStruct((width, width), f32),
            jax.ShapeDtypeStruct((8, BLOCK), f32),
        ),
        in_specs=[vmem] * 5,
        out_specs=(vmem, vmem, vmem),
        scratch_shapes=[
            pltpu.VMEM((width, rows_dev), bf16),
            pltpu.VMEM((CHUNKS, 4, 2, chunk, BLOCK), bf16),
            pltpu.VMEM((CHUNKS, 4, 2, chunk, BLOCK), f32),
            pltpu.VMEM((CHUNKS, 4, 2, chunk, BLOCK), bf16),
            pltpu.VMEM((CHUNKS, 3, 2, chunk, BLOCK), bf16),
            pltpu.VMEM((width, rows_dev), f32),
            pltpu.VMEM((CHUNKS, 2, 16, pieces, chunk), f32),
            pltpu.VMEM((CHUNKS, 16, pieces, chunk), f32),
            pltpu.VMEM((CHUNKS, 16, pieces, chunk), f32),
            pltpu.VMEM((CHUNKS, 15, pieces, chunk), f32),
            pltpu.VMEM((CHUNKS, 8, pieces, chunk), f32),
            pltpu.VMEM((CHUNKS, 2, 16, pieces, chunk), f32),
            pltpu.VMEM((16, 8, BLOCK), f32),
            pltpu.VMEM((8, 8, BLOCK), f32),
            pltpu.VMEM((2, 8, BLOCK), f32),
        ] + [dma((CHUNKS,))] * 14 + [dma((3,))] * 2,
        compiler_params=pltpu.CompilerParams(
            collective_id=1, has_side_effects=True, vmem_limit_bytes=limit
        ),
    )(own, send, features, weight, bias_rows)
    return fg, wg, bias.reshape(-1)[:width]


def solution(mesh):
    placed = (
        P(("row", "col"), None),
        P(("row", "col"), None),
        P(("row", "col"), None),
        P(),
        P("row", "col", None),
        P("row", "col", None),
        P("row", "col", None, None, None),
        P("row", "col"),
    )
    return jax.shard_map(
        local,
        mesh=mesh,
        in_specs=placed,
        out_specs=(P(("row", "col"), None), P(), P()),
        check_vma=False,
    )
```

time: 730 us -> 167 us (0.23)
  waiting for transfers between devices: 373 us -> 0 us
  Pallas kernels: 0 us -> 160 us
  other arithmetic: 151 us -> 0 us
  blocking collectives: 80.3 us -> 0 us
  matrix products: 53.3 us -> 0 us
  local copies, waits for them, and re-layouts: 53.9 us -> 5.19 us
  between operations: 13.8 us -> 1.3 us
    psum x1 -> x0, waiting for transfers between devices: 176 us -> none  [local(): lax.psum((local_weight, local_bias), ('row', 'col'))]
    pallas_call x0 -> x4, Pallas kernels: none -> 160 us  [the longest x1 86.2 us: local(): pl.pallas_call(functools.partial(reduce_body, 1.0 / math.sqrt(vertices)),...]
    all_gather x1 -> x0, waiting for transfers between devices: 145 us -> none  [local(): grad_panel = lax.all_gather(masked, 'col', axis=0, tiled=True)]
    scatter-add x4 -> x0, other arithmetic: 145 us -> none  [add_tiles(): jax.ops.segment_sum(products, cols_now, num_segments=col_blocks)]
    psum x1 -> x0, blocking collectives: 80.3 us -> none  [local(): lax.psum((local_weight, local_bias), ('row', 'col'))]
    dot_general x6 -> x0, matrix products: 53.3 us -> none  [the longest x4 48.6 us: add_tiles(): jnp.einsum('kab,kaf->kbf', vals_now, gathered, preferred_element_type=jnp...]
    reduce_scatter x1 -> x0, waiting for transfers between devices: 51.8 us -> none  [local(): lax.psum_scatter(partial_sum, 'row', scatter_dimension=0, tiled=True)]
    gather x4 -> x0, local copies, waits for them, and re-layouts: 35.6 us -> none  [add_tiles(): gathered = jnp.take(grad_blocks, rows_now, axis=0)]
  transfers between devices with their start and end apart: 3 -> 0, of which waited for: 3 -> 0; matrix products, arithmetic and copies ran while one was open for 2% -> 0% of each run, Pallas kernels for 0% -> 0%
where the time goes in v1:
time: 167 us; the launch traced here: 166 us
  Pallas kernels  160 us (96%)
  local copies, waits for them, and re-layouts  5.19 us (3%)
    pallas_call x1, Pallas kernels, local(): pl.pallas_call(functools.partial(reduce_body, 1.0 / math.sqrt(vertices)),...  86.2 us
    pallas_call x1, Pallas kernels, local(): pl.pallas_call(gather_body, out_shape=(jax.ShapeDtypeStruct((AG_CHUNKS, 6...  60.5 us
    pallas_call x1, Pallas kernels, local(): pl.pallas_call(product_body, out_shape=(jax.ShapeDtypeStruct((CHUNKS, 4,...  11.4 us
    unnamed x2, local copies, waits for them, and re-layouts  3.93 us

profile of v1, /device:TPU:1, one launch (start us, length us, event | category | flops | bytes accessed | tf_op | source)
XLA Modules:
  0.0 166.3 jit_solution(7761586501729242546)
XLA Ops:
  1.3 1.8 %shard_map.103.meta_s = s32[8,384]{1,0:T(8,128)} custom-call(s32[1,256]{1,0:T(1,128)} %bitcast.6, s32[1,256]{1,0:T(1,128)} %bitcast.7, s32[1,1]{1,0:T(1,128)S(6)} %copy.13.count), custom_call_target="tpu_custom_call" | custom-call | tf_op jit(solution)/shard_map/pallas_call | solution.py:524
  3.0 60.5 %shard_map.104 = (bf16[2,64,256,128]{3,2,1,0:T(8,128)(2,1)}, f32[1,512]{1,0:T(1,128)}) custom-call(bf16[256,512]{1,0:T(8,128)(2,1)} %pre.1, bf16[256,512]{1,0:T(8,128)(2,1)} %cot.1), custom_call_target="tpu_custom_call" | custom-call | tf_op jit(solution)/shard_map/pallas_call | solution.py:508
  63.6 11.4 %shard_map.105 = (f32[4,4,2,128,128]{4,3,2,1,0:T(8,128)}, bf16[4,4,2,128,128]{4,3,2,1,0:T(8,128)(2,1)}) custom-call(s32[8,384]{1,0:T(8,128)} %shard_map.103.meta_s, bf16[2,64,256,128]{3,2,1,0:T(8,128)(2,1)} %get-tuple-element.10.panel, bf16[256,128,128]{2,1,0:T(8,128)(2,1)} %bitcast.5), custom_call_target="tpu_custom_call" | custom-call | tf_op jit(solution)/shard_map/pallas_call | solution.py:532
  75.0 86.2 %shard_map.106 = (bf16[256,512]{1,0:T(8,128)(2,1)}, f32[512,512]{1,0:T(8,128)}, f32[8,128]{1,0:T(8,128)}) custom-call(f32[4,4,2,128,128]{4,3,2,1,0:T(8,128)} %get-tuple-element.11.own, bf16[4,4,2,128,128]{4,3,2,1,0:T(8,128)(2,1)} %get-tuple-element.12.send1, bf16[256,512]{1,0:T(8,128)(2,1)} %feat.1, bf16[512,512]{1,0:T(8,128)(2,1)} %weight.1, ...), custom_call_target="tpu_custom_call" | custom-call | tf_op jit(solution)/shard_map/pallas_call | solution.py:554
  161.1 1.3 slice_bitcast_fusion
  162.4 1.7 %copy.14 = bf16[256,512]{1,0:T(8,128)(2,1)} copy(bf16[256,512]{1,0:T(8,128)(2,1)} %get-tuple-element.20) | data formatting | bytes 524288
  164.1 2.3 %copy.15 = f32[512,512]{1,0:T(8,128)} copy(f32[512,512]{1,0:T(8,128)} %get-tuple-element.21) | data formatting | bytes 2097152

commit v2 on v1

v2 whole, which is shorter than its diff:
```python
import functools
import math

import jax
import jax.numpy as jnp
from jax import lax
from jax.experimental import pallas as pl
from jax.experimental.pallas import tpu as pltpu
from jax.sharding import PartitionSpec as P

AG_CHUNKS = 2
BLOCK = 128
MESH = pl.DeviceIdType.MESH


def gather_body(
    pre, cot, feat, trow, tcol, count, panel, feat_all, bias_out, meta_v,
    own_blocks, own_feat, ag_send, ag_recv, own_sem, f_send, f_recv
):
    rows_dev, width = pre.shape
    chunk = width // AG_CHUNKS
    half_chunk = chunk // 2

    r = lax.axis_index("row")
    c = lax.axis_index("col")
    zl, core = r // 2, r % 2
    zh, m = c // 16, c % 16
    y, x = m // 4, m % 4
    w8 = zh * 4 + zl
    partner = (r + 1 - 2 * core, c)
    z_partner = (r, (1 - zh) * 16 + m)

    def plane_peer(d):
        return (r, zh * 16 + (m + d) % 16)

    def z_peer(d):
        q = (w8 + d) % 8
        return (2 * (q % 4) + core, (q // 4) * 16 + m)

    def z_near(d):
        return (2 * ((zl + d) % 4) + core, c)

    def neighbour(dim, d):
        if dim == 0:
            return (r, zh * 16 + y * 4 + (x + d) % 4)
        return (r, zh * 16 + ((y + d) % 4) * 4 + x)

    def remote(src, dst, send_sem, recv_sem, device):
        return pltpu.make_async_remote_copy(
            src_ref=src, dst_ref=dst, send_sem=send_sem, recv_sem=recv_sem,
            device_id=device, device_id_type=MESH,
        )

    def wait_recv(ref, send_sem, recv_sem):
        remote(ref, ref, send_sem, recv_sem, partner).wait_recv()

    def wait_send(ref, send_sem, recv_sem):
        remote(ref, ref, send_sem, recv_sem, partner).wait_send()

    barrier = pltpu.get_barrier_semaphore()
    for device in (
        z_partner, neighbour(0, 1), neighbour(0, -1), neighbour(1, 1), neighbour(1, -1),
        z_near(1), z_near(2), z_near(3),
    ):
        pl.semaphore_signal(barrier, inc=1, device_id=device, device_id_type=MESH)

    def block_of(plane, d1, d2, h):
        if h == 0:
            xx, yy = (x + d1) % 4, (y + d2) % 4
        else:
            xx, yy = (x + d2) % 4, (y + d1) % 4
        return 2 * (plane * 16 + yy * 4 + xx) + h

    def ag_copy(k, b, device, part=None, h=None):
        ref = panel.at[k, b]
        if part is not None:
            ref = panel.at[k, b, pl.ds(part * half_chunk, half_chunk)]
        src = ref if h is None else own_blocks.at[k, h]
        remote(src, ref, ag_send.at[k], ag_recv.at[k, b], device).start()

    def ag_wait(k, b):
        wait_recv(panel.at[k, b], ag_send.at[k], ag_recv.at[k, b])

    def first_dim(h):
        return 0 if h == 0 else 1

    def second_dim(h):
        return 1 if h == 0 else 0

    def s0(k, plane, mine):
        for dim in (first_dim, second_dim):
            for h in (0, 1):
                b = block_of(plane, 0, 0, h)
                for d in (1, -1):
                    ag_copy(k, b, neighbour(dim(h), d), None, h if mine else None)

    def s1(k, plane):
        for d in (-1, 1):
            for h in (0, 1):
                b = block_of(plane, d, 0, h)
                ag_wait(k, b)
                ag_copy(k, b, neighbour(first_dim(h), -d), 0 if d == -1 else 1)
                for e in (1, -1):
                    ag_copy(k, b, neighbour(second_dim(h), e))

    def s2(k, plane):
        for h in (0, 1):
            b = block_of(plane, 2, 0, h)
            ag_wait(k, b)
            for e in (1, -1):
                ag_copy(k, b, neighbour(second_dim(h), e))

    def s3(k, plane):
        for d1 in (0, -1, 1, 2):
            for d in (-1, 1):
                for h in (0, 1):
                    b = block_of(plane, d1, d, h)
                    ag_wait(k, b)
                    ag_copy(k, b, neighbour(second_dim(h), -d), 0 if d == -1 else 1)

    def s4(k, plane):
        for d1 in (0, -1, 1, 2):
            for h in (0, 1):
                ag_wait(k, block_of(plane, d1, 2, h))

    def z_go(k):
        for h in (0, 1):
            b = block_of(zh, 0, 0, h)
            ag_copy(k, b, z_partner, None, h)

    def z_come(k):
        for h in (0, 1):
            ag_wait(k, block_of(1 - zh, 0, 0, h))
        s0(k, 1 - zh, False)

    places = []

    def prepare(k):
        lanes = pl.ds(k * chunk, chunk)
        kept = jnp.where(
            pre[:, lanes].astype(jnp.float32) > 0, cot[:, lanes].astype(jnp.float32), 0.0
        )
        for h in (0, 1):
            part = kept[h * BLOCK:(h + 1) * BLOCK, :]
            own_blocks[k, h] = part.T.astype(jnp.bfloat16)
        place = pltpu.make_async_copy(
            own_blocks.at[k], panel.at[k, pl.ds(2 * c, 2)], own_sem.at[k]
        )
        place.start()
        places.append(place)
        return jnp.sum(kept, axis=0, keepdims=True)

    def order_tiles():
        n_tiles = trow.shape[1]
        n_cols = 16
        lane = lax.broadcasted_iota(jnp.int32, (n_tiles, n_tiles), 1)
        sub = lax.broadcasted_iota(jnp.int32, (n_tiles, n_tiles), 0)
        live = count[0, 0]
        lane1 = lax.broadcasted_iota(jnp.int32, (1, n_tiles), 1)
        col_r = jnp.where(lane1 < live, tcol[...], 100)
        diag = lane == sub
        col_c = jnp.sum(jnp.where(diag, col_r, 0), axis=1, keepdims=True)
        row_c = jnp.sum(jnp.where(diag, trow[...], 0), axis=1, keepdims=True)
        rank_c = jnp.sum(
            jnp.where((col_r == col_c) & (lane < sub), 1, 0), axis=1, keepdims=True
        )
        lane_j = lax.broadcasted_iota(jnp.int32, (n_tiles, BLOCK), 1)
        n_r = jnp.sum(jnp.where(col_c == lane_j, 1, 0), axis=0, keepdims=True)
        lane_j1 = lax.broadcasted_iota(jnp.int32, (1, BLOCK), 1)
        pad_r = jnp.where(lane_j1 < n_cols, n_r + (n_r & 1), 0)
        base_c = jnp.sum(jnp.where(lane_j < col_c, pad_r, 0), axis=1, keepdims=True)
        pos_c = jnp.where(col_c < n_cols, base_c + rank_c, 100000)
        jj_lane = lax.broadcasted_iota(jnp.int32, (BLOCK, BLOCK), 1)
        jj_sub = lax.broadcasted_iota(jnp.int32, (BLOCK, BLOCK), 0)
        pad_c = jnp.sum(jnp.where(jj_lane == jj_sub, pad_r, 0), axis=1, keepdims=True)
        end_r = jnp.sum(jnp.where(jj_sub <= jj_lane, pad_c, 0), axis=0, keepdims=True)
        last_r = jnp.maximum(end_r // 2 - 1, 0)
        has_r = jnp.where(n_r > 0, 1, 0)
        meta_w = meta_v.shape[1]
        lane_p = lax.broadcasted_iota(jnp.int32, (n_tiles, meta_w), 1)
        sub_p = lax.broadcasted_iota(jnp.int32, (n_tiles, meta_w), 0)
        hit = lane_p == pos_c
        meta_v[...] = jnp.zeros(meta_v.shape, jnp.int32)
        meta_v[0:1, :] = n_tiles + jnp.sum(
            jnp.where(hit, sub_p - n_tiles, 0), axis=0, keepdims=True
        )
        meta_v[1:2, :] = jnp.sum(jnp.where(hit, row_c, 0), axis=0, keepdims=True)
        meta_v[2:3, :] = 1 - jnp.sum(jnp.where(hit & (rank_c == 0), 1, 0), axis=0, keepdims=True)
        meta_v[3:4, 0:BLOCK] = last_r
        meta_v[4:5, 0:BLOCK] = has_r
        meta_v[5:6, 0:BLOCK] = jnp.sum(pad_r, axis=1, keepdims=True) // 2 + 0 * lane_j1

    bias_rows = [prepare(0)]
    pl.semaphore_wait(barrier, 8)
    s0(0, zh, True)
    z_go(0)
    for k in range(1, AG_CHUNKS):
        bias_rows.append(prepare(k))
        s0(k, zh, True)
        z_go(k)
    bias_out[...] = jnp.concatenate(bias_rows, axis=1)
    own_feat[...] = feat[...].astype(jnp.float32).T.astype(jnp.bfloat16)
    for d in (1, 2, 3):
        remote(own_feat, feat_all.at[zl], f_send.at[0], f_recv.at[0], z_near(d)).start()
    place = pltpu.make_async_copy(own_feat, feat_all.at[zl], f_send.at[1])
    place.start()
    places.append(place)
    order_tiles()
    for k in range(AG_CHUNKS):
        s1(k, zh)
        s2(k, zh)
        if k > 0:
            s3(k - 1, 1 - zh)
            s4(k - 1, zh)
            s4(k - 1, 1 - zh)
        z_come(k)
        s3(k, zh)
        s1(k, 1 - zh)
        s2(k, 1 - zh)
    k = AG_CHUNKS - 1
    s3(k, 1 - zh)
    s4(k, zh)
    s4(k, 1 - zh)
    for place in places:
        place.wait()
    for k in range(AG_CHUNKS):
        wait_send(panel.at[k, pl.ds(0, 62)], ag_send.at[k], ag_recv.at[k, 0])
    wait_recv(feat_all.at[pl.ds(0, 3)], f_send.at[0], f_recv.at[0])
    wait_send(feat_all.at[pl.ds(0, 3)], f_send.at[0], f_recv.at[0])


def product_body(meta_s, panel, vals, own, send, slots):
    chunk = panel.shape[1]
    core = lax.axis_index("row") % 2
    pairs = meta_s[5, 0]

    def step(p, acc):
        lhs = jnp.concatenate(
            [panel[meta_s[1, 2 * p]], panel[meta_s[1, 2 * p + 1]]], axis=1
        )
        both = [
            vals[jnp.minimum(meta_s[0, 2 * p + i], vals.shape[0] - 1)] for i in (0, 1)
        ]
        alive = (meta_s[0, 2 * p + 1] < vals.shape[0]).astype(jnp.int32).astype(jnp.bfloat16)
        rhs = jnp.concatenate([both[0], both[1] * alive], axis=0)
        keep = meta_s[2, 2 * p].astype(jnp.float32)
        acc = acc * keep + jnp.dot(lhs, rhs, preferred_element_type=jnp.float32)
        slots[p] = acc
        return acc

    def several(g, acc):
        for i in range(8):
            acc = step(8 * g + i, acc)
        return acc

    lax.fori_loop(0, (pairs + 7) // 8, several, jnp.zeros((chunk, BLOCK), jnp.float32))

    def column(j):
        return slots[meta_s[3, j]] * meta_s[4, j].astype(jnp.float32)

    for q in range(4):
        for h in (0, 1):
            lanes = slice(h * BLOCK, (h + 1) * BLOCK)
            send[q, :, lanes] = column(2 * (2 * q + 1 - core) + h).astype(jnp.bfloat16)
            own[q, :, lanes] = column(2 * (2 * q + core) + h)


def reduce_body(
    norm_scale,
    own, send1, feat_all, weight, bias_in,
    fg_out, gathered, bias_out,
    recv1, total, send2, recv2, ar, recv_p, xs, recv_xy, zbuf, bxy, bz, bp,
    rs_send1, rs_recv1, rs_send2, rs_recv2, small_send, small_recv, b_send, b_recv,
):
    width = feat_all.shape[1]
    half = width // 2

    r = lax.axis_index("row")
    c = lax.axis_index("col")
    zl, core = r // 2, r % 2
    zh, m = c // 16, c % 16
    y, x = m // 4, m % 4
    w8 = zh * 4 + zl
    partner = (r + 1 - 2 * core, c)
    z_partner = (r, (1 - zh) * 16 + m)

    def plane_peer(d):
        return (r, zh * 16 + (m + d) % 16)

    def z_peer(d):
        q = (w8 + d) % 8
        return (2 * (q % 4) + core, (q // 4) * 16 + m)

    def z_near(d):
        return (2 * ((zl + d) % 4) + core, c)

    def neighbour(dim, d):
        if dim == 0:
            return (r, zh * 16 + y * 4 + (x + d) % 4)
        return (r, zh * 16 + ((y + d) % 4) * 4 + x)

    def remote(src, dst, send_sem, recv_sem, device):
        return pltpu.make_async_remote_copy(
            src_ref=src, dst_ref=dst, send_sem=send_sem, recv_sem=recv_sem,
            device_id=device, device_id_type=MESH,
        )

    def wait_recv(ref, send_sem, recv_sem):
        remote(ref, ref, send_sem, recv_sem, partner).wait_recv()

    def wait_send(ref, send_sem, recv_sem):
        remote(ref, ref, send_sem, recv_sem, partner).wait_send()

    barrier = pltpu.get_barrier_semaphore()

    def greet(device):
        pl.semaphore_signal(barrier, inc=1, device_id=device, device_id_type=MESH)

    greet(partner)

    def greet_plane(d, carry):
        greet(plane_peer(d))
        return carry

    def greet_z(d, carry):
        greet(z_peer(d))
        return carry

    lax.fori_loop(1, 16, greet_plane, 0)
    lax.fori_loop(1, 8, greet_z, 0)
    bias_local = bias_in[...]
    bxy[m] = jnp.zeros(bxy.shape[1:], jnp.float32)
    for q in range(width // BLOCK):
        bxy[m, pl.ds(q, 1)] = bias_local[:, q * BLOCK:(q + 1) * BLOCK]

    def bias_plane(d, carry):
        remote(bxy.at[m], bxy.at[m], b_send.at[0], b_recv.at[0], plane_peer(d)).start()
        return carry

    def bias_z(d, carry):
        remote(bz.at[w8], bz.at[w8], b_send.at[1], b_recv.at[1], z_peer(d)).start()
        return carry

    pl.semaphore_wait(barrier, 23)

    order = [(zl + d) % 4 for d in (1, 2, 3, 0)]
    for q in order:
        remote(
            send1.at[q], recv1.at[q], rs_send1.at[q], rs_recv1.at[q], partner
        ).start()
    lax.fori_loop(1, 16, bias_plane, 0)
    for i, q in enumerate(order):
        wait_recv(recv1.at[q], rs_send1.at[q], rs_recv1.at[q])
        pair = own[q] + recv1[q].astype(jnp.float32)
        send2[q] = pair.astype(jnp.bfloat16)
        if i < 3:
            remote(
                send2.at[q], recv2.at[i], rs_send2.at[i], rs_recv2.at[i], z_near(i + 1)
            ).start()
        else:
            total[...] = pair

    def term(which):
        rows = pl.ds(which * half, half)
        acc = None
        for q in order:
            piece = lax.dot_general(
                feat_all[q, rows, :], send2[q], (((1,), (1,)), ((), ())),
                preferred_element_type=jnp.float32,
            )
            acc = piece if acc is None else acc + piece
        return acc.reshape(recv_p.shape)

    ar[...] = term(1 - core)
    remote(ar, recv_p, small_send.at[0], small_recv.at[0], partner).start()
    mine = term(core)
    wait_recv(recv_p, small_send.at[0], small_recv.at[0])
    xs[...] = mine + recv_p[...]

    def go_xy(d, carry):
        remote(
            xs.at[(m + d) % 16], recv_xy.at[d - 1],
            small_send.at[1], small_recv.at[1], plane_peer(d),
        ).start()
        return carry

    lax.fori_loop(1, 16, go_xy, 0)

    wait_recv(bxy.at[pl.ds(0, 15)], b_send.at[0], b_recv.at[0])
    plane_sum = bxy[0]
    for i in range(1, 16):
        plane_sum = plane_sum + bxy[i]
    bz[w8] = plane_sum
    lax.fori_loop(1, 8, bias_z, 0)

    wait_recv(recv_xy, small_send.at[1], small_recv.at[1])
    zbuf[w8] = (xs[m] + jnp.sum(recv_xy[...], axis=0)).astype(zbuf.dtype)

    def go_z(d, carry):
        remote(
            zbuf.at[w8], zbuf.at[w8], small_send.at[2], small_recv.at[2], z_peer(d)
        ).start()
        return carry

    lax.fori_loop(1, 8, go_z, 0)

    wait_recv(bz.at[pl.ds(0, 7)], b_send.at[1], b_recv.at[1])
    z_sum = bz[0]
    for i in range(1, 8):
        z_sum = z_sum + bz[i]
    bp[0] = z_sum
    remote(bp.at[0], bp.at[1], b_send.at[2], b_recv.at[2], partner).start()

    wait_recv(zbuf.at[pl.ds(0, 7)], small_send.at[2], small_recv.at[2])
    grad = zbuf[0].astype(jnp.float32)
    for i in range(1, 8):
        grad = grad + zbuf[i].astype(jnp.float32)
    gathered[core, m] = grad * norm_scale

    def go_g(d, carry):
        ref = gathered.at[core, m]
        remote(ref, ref, small_send.at[3], small_recv.at[3], plane_peer(d)).start()
        return carry

    lax.fori_loop(1, 16, go_g, 0)

    summed = total[...]
    for d in range(3):
        wait_recv(recv2.at[d], rs_send2.at[d], rs_recv2.at[d])
        summed = summed + recv2[d].astype(jnp.float32)
    fg_out[...] = jnp.dot(
        weight[...], summed.astype(jnp.bfloat16), preferred_element_type=jnp.float32
    ).T.astype(jnp.bfloat16)
    wait_recv(bp.at[1], b_send.at[2], b_recv.at[2])
    bias_out[...] = (bp[0] + bp[1]) * norm_scale

    wait_recv(gathered.at[0, pl.ds(0, 15)], small_send.at[3], small_recv.at[3])
    ref = gathered.at[core]
    remote(ref, ref, small_send.at[4], small_recv.at[4], partner).start()
    for q in range(4):
        wait_send(send1.at[q], rs_send1.at[q], rs_recv1.at[q])
    for d in range(3):
        wait_send(recv2.at[d], rs_send2.at[d], rs_recv2.at[d])
    wait_send(ar, small_send.at[0], small_recv.at[0])
    wait_send(recv_xy, small_send.at[1], small_recv.at[1])
    wait_send(zbuf.at[pl.ds(0, 7)], small_send.at[2], small_recv.at[2])
    wait_send(gathered.at[0, pl.ds(0, 15)], small_send.at[3], small_recv.at[3])
    wait_send(bxy.at[pl.ds(0, 15)], b_send.at[0], b_recv.at[0])
    wait_send(bz.at[pl.ds(0, 7)], b_send.at[1], b_recv.at[1])
    wait_send(bp.at[0], b_send.at[2], b_recv.at[2])
    wait_recv(gathered.at[0], small_send.at[4], small_recv.at[4])
    wait_send(gathered.at[0], small_send.at[4], small_recv.at[4])


def finish_body(fg, wg, bias, fg_out, wg_out, bias_out):
    fg_out[...] = fg[...]
    wg_out[...] = wg[...]
    for q in range(bias_out.shape[0] // BLOCK):
        bias_out[pl.ds(q * BLOCK, BLOCK)] = bias[q]


def local(features, pre_act, out_grad, weight, tile_rows, tile_cols, tile_vals, tile_counts):
    rows_dev, width = features.shape
    slots = tile_rows.shape[2]
    ag_chunk = width // AG_CHUNKS
    n_pairs = (slots + 16) // 2 + 8
    piece = (width // 32, width)
    vertices = rows_dev * lax.axis_size("row") * lax.axis_size("col")
    bf16, f32 = jnp.bfloat16, jnp.float32
    shape = jax.ShapeDtypeStruct
    vmem = pl.BlockSpec(memory_space=pltpu.VMEM)
    smem = pl.BlockSpec(memory_space=pltpu.SMEM)
    anywhere = pl.BlockSpec(memory_space=pl.ANY)
    dma = pltpu.SemaphoreType.DMA
    limit = 56 * 1024 * 1024
    panel, feat_all, bias_rows, meta = pl.pallas_call(
        gather_body,
        out_shape=(
            shape((AG_CHUNKS, 64, ag_chunk, BLOCK), bf16),
            shape((4, width, rows_dev), bf16),
            shape((1, width), f32),
            shape((8, 384), jnp.int32),
        ),
        in_specs=[vmem] * 5 + [smem],
        out_specs=(anywhere, anywhere, vmem, vmem),
        scratch_shapes=[
            pltpu.VMEM((AG_CHUNKS, 2, ag_chunk, BLOCK), bf16),
            pltpu.VMEM((width, rows_dev), bf16),
            dma((AG_CHUNKS,)), dma((AG_CHUNKS, 64)), dma((AG_CHUNKS,)), dma((2,)), dma((1,)),
        ],
        compiler_params=pltpu.CompilerParams(
            collective_id=0, has_side_effects=True, vmem_limit_bytes=limit
        ),
    )(
        pre_act, out_grad, features,
        tile_rows.reshape(1, slots), tile_cols.reshape(1, slots), tile_counts.reshape(1, 1),
    )
    out_block = pl.BlockSpec((4, ag_chunk, rows_dev), lambda k, meta: (0, k, 0))
    own, send = pl.pallas_call(
        product_body,
        out_shape=(shape((4, width, rows_dev), f32), shape((4, width, rows_dev), bf16)),
        grid_spec=pltpu.PrefetchScalarGridSpec(
            num_scalar_prefetch=1,
            grid=(AG_CHUNKS,),
            in_specs=[
                pl.BlockSpec((None, 64, ag_chunk, BLOCK), lambda k, meta: (k, 0, 0, 0)),
                pl.BlockSpec((slots, BLOCK, BLOCK), lambda k, meta: (0, 0, 0)),
            ],
            out_specs=(out_block, out_block),
            scratch_shapes=[pltpu.VMEM((n_pairs, ag_chunk, BLOCK), f32)],
        ),
        compiler_params=pltpu.CompilerParams(vmem_limit_bytes=limit),
    )(meta, panel, tile_vals.reshape(slots, BLOCK, BLOCK))
    fg, wg, bias = pl.pallas_call(
        functools.partial(reduce_body, 1.0 / math.sqrt(vertices)),
        out_shape=(
            shape((rows_dev, width), bf16),
            shape((2, 16) + piece, f32),
            shape((8, BLOCK), f32),
        ),
        in_specs=[vmem] * 5,
        out_specs=(vmem, vmem, vmem),
        scratch_shapes=[
            pltpu.VMEM((4, width, rows_dev), bf16),
            pltpu.VMEM((width, rows_dev), f32),
            pltpu.VMEM((4, width, rows_dev), bf16),
            pltpu.VMEM((3, width, rows_dev), bf16),
            pltpu.VMEM((16,) + piece, f32),
            pltpu.VMEM((16,) + piece, f32),
            pltpu.VMEM((16,) + piece, f32),
            pltpu.VMEM((15,) + piece, f32),
            pltpu.VMEM((8,) + piece, bf16),
            pltpu.VMEM((16, 8, BLOCK), f32),
            pltpu.VMEM((8, 8, BLOCK), f32),
            pltpu.VMEM((2, 8, BLOCK), f32),
            dma((4,)), dma((4,)), dma((3,)), dma((3,)), dma((5,)), dma((5,)), dma((3,)), dma((3,)),
        ],
        compiler_params=pltpu.CompilerParams(
            collective_id=1, has_side_effects=True, vmem_limit_bytes=limit
        ),
    )(own, send, feat_all, weight, bias_rows)
    return pl.pallas_call(
        finish_body,
        out_shape=(shape((rows_dev, width), bf16), shape((width, width), f32), shape((width,), f32)),
        in_specs=[vmem] * 3,
        out_specs=(vmem, vmem, vmem),
    )(fg, wg.reshape(width, width), bias)


def solution(mesh):
    placed = (
        P(("row", "col"), None),
        P(("row", "col"), None),
        P(("row", "col"), None),
        P(),
        P("row", "col", None),
        P("row", "col", None),
        P("row", "col", None, None, None),
        P("row", "col"),
    )
    return jax.shard_map(
        local,
        mesh=mesh,
        in_specs=placed,
        out_specs=(P(("row", "col"), None), P(), P()),
        check_vma=False,
    )
```

time: 167 us -> 143 us (0.86)
  Pallas kernels: 160 us -> 141 us
  local copies, waits for them, and re-layouts: 5.19 us -> 0 us
    pallas_call x1, Pallas kernels: 86.2 us -> 68.3 us  [local(): pl.pallas_call(functools.partial(reduce_body, 1.0 / math.sqrt(vertices)),...]
    unnamed x2 -> x0, local copies, waits for them, and re-layouts: 3.93 us -> none
where the time goes in v2:
time: 143 us; the launch traced here: 142 us
  Pallas kernels  141 us (99%)
    pallas_call x1, Pallas kernels, local(): pl.pallas_call(functools.partial(reduce_body, 1.0 / math.sqrt(vertices)),...  68.3 us
    pallas_call x1, Pallas kernels, local(): pl.pallas_call(gather_body, out_shape=(shape((AG_CHUNKS, 64, ag_chunk, BL...  60.8 us
    pallas_call x1, Pallas kernels, local(): pl.pallas_call(product_body, out_shape=(shape((4, width, rows_dev), f32),...  9.7 us

profile of v2, /device:TPU:1, one launch (start us, length us, event | category | flops | bytes accessed | tf_op | source)
XLA Modules:
  0.0 142.4 jit_solution(2753301841179021173)
XLA Ops:
  1.3 60.8 %shard_map.103 = (bf16[2,64,256,128]{3,2,1,0:T(8,128)(2,1)}, bf16[4,512,256]{2,1,0:T(8,128)(2,1)}, f32[1,512]{1,0:T(1,128)}, s32[8,384]{1,0:T(8,128)}) custom-call(bf16[256,512]{1,0:T(8,128)(2,1)} %pre.1, bf16[256,512]{1,0:T(8,128)(2,1)} %cot.1, bf16[256,512]{1,0:T(8,128)(2,1)} %feat.1, s32[1,256]{1,0:T(1,128)} %bitcast.6, s32[1,256]{1,0:T(1,128)} %bitcast.7, ...), custom_call_target="tpu_custom_call" | custom-call | tf_op jit(solution)/shard_map/pallas_call | solution.py:476
  62.1 9.7 %shard_map.104 = (f32[4,512,256]{2,1,0:T(8,128)}, bf16[4,512,256]{2,1,0:T(8,128)(2,1)}) custom-call(s32[8,384]{1,0:T(8,128)} %get-tuple-element.12.meta_s, bf16[2,64,256,128]{3,2,1,0:T(8,128)(2,1)} %get-tuple-element.13.panel, bf16[256,128,128]{2,1,0:T(8,128)(2,1)} %bitcast.4), custom_call_target="tpu_custom_call" | custom-call | tf_op jit(solution)/shard_map/pallas_call | solution.py:499
  71.8 68.3 %shard_map.105 = (bf16[256,512]{1,0:T(8,128)(2,1)}, f32[2,16,16,512]{3,2,1,0:T(8,128)}, f32[8,128]{1,0:T(8,128)}) custom-call(f32[4,512,256]{2,1,0:T(8,128)} %get-tuple-element.14.own, bf16[4,512,256]{2,1,0:T(8,128)(2,1)} %get-tuple-element.15.send1, bf16[4,512,256]{2,1,0:T(8,128)(2,1)} %get-tuple-element.16.feat_all, bf16[512,512]{1,0:T(8,128)(2,1)} %weight.1, ...), custom_call_target="tpu_custom_call" | custom-call | tf_op jit(solution)/shard_map/pallas_call | solution.py:514
  140.1 2.4 %shard_map.106 = (bf16[256,512]{1,0:T(8,128)(2,1)}, f32[512,512]{1,0:T(8,128)}, f32[512]{0:T(512)}) custom-call(bf16[256,512]{1,0:T(8,128)(2,1)} %get-tuple-element.18.fg, f32[512,512]{1,0:T(8,128)} %bitcast.5, f32[8,128]{1,0:T(8,128)} %get-tuple-element.20.bias), custom_call_target="tpu_custom_call" | custom-call | tf_op jit(solution)/shard_map/pallas_call | solution.py:542

commit v3 on v0

v3 whole, which is shorter than its diff:
```python
import functools
import math

import jax
import jax.numpy as jnp
from jax import lax
from jax.experimental import pallas as pl
from jax.experimental.pallas import tpu as pltpu
from jax.sharding import PartitionSpec as P

CHUNKS = 2
BLOCK = 128
MESH = pl.DeviceIdType.MESH


def body(
    norm_scale,
    pre, cot, feat, weight, trow, tcol, count, vals_hbm,
    fg_out, gathered, bias_out,
    panel0, panel1, vals, slots, feat_all, own, send1, recv1, total, send2, recv2, fg_acc,
    ar, recv_p, xs, recv_xy, zbuf, bxy, bz, bp, meta_v, meta_s,
    local_sem, ag_send, ag_recv, f_send, f_recv, rs_send1, rs_recv1, rs_send2, rs_recv2,
    ar_send, ar_recv, b_send, b_recv,
):
    rows_dev, width = pre.shape
    chunk = width // CHUNKS
    half_chunk = chunk // 2
    half = width // 2
    n_pairs = slots.shape[0]
    n_tiles = vals_hbm.shape[0]
    n_cols = 16
    panel = (panel0, panel1)

    r = lax.axis_index("row")
    c = lax.axis_index("col")
    zl, core = r // 2, r % 2
    zh, m = c // 16, c % 16
    y, x = m // 4, m % 4
    w8 = zh * 4 + zl
    partner = (r + 1 - 2 * core, c)
    z_partner = (r, (1 - zh) * 16 + m)

    def plane_peer(d):
        return (r, zh * 16 + (m + d) % 16)

    def z_peer(d):
        q = (w8 + d) % 8
        return (2 * (q % 4) + core, (q // 4) * 16 + m)

    def z_near(d):
        return (2 * ((zl + d) % 4) + core, c)

    def neighbour(dim, d):
        if dim == 0:
            return (r, zh * 16 + y * 4 + (x + d) % 4)
        return (r, zh * 16 + ((y + d) % 4) * 4 + x)

    def remote(src, dst, send_sem, recv_sem, device):
        return pltpu.make_async_remote_copy(
            src_ref=src, dst_ref=dst, send_sem=send_sem, recv_sem=recv_sem,
            device_id=device, device_id_type=MESH,
        )

    def wait_recv(ref, send_sem, recv_sem):
        remote(ref, ref, send_sem, recv_sem, partner).wait_recv()

    def wait_send(ref, send_sem, recv_sem):
        remote(ref, ref, send_sem, recv_sem, partner).wait_send()

    tiles_copy = pltpu.make_async_copy(
        vals_hbm, vals.at[pl.ds(0, n_tiles)], local_sem.at[0]
    )
    tiles_copy.start()
    barrier = pltpu.get_barrier_semaphore()

    def greet(device):
        pl.semaphore_signal(barrier, inc=1, device_id=device, device_id_type=MESH)

    greet(partner)

    def greet_plane(d, carry):
        greet(plane_peer(d))
        return carry

    def greet_z(d, carry):
        greet(z_peer(d))
        return carry

    lax.fori_loop(1, 16, greet_plane, 0)
    lax.fori_loop(1, 8, greet_z, 0)

    def block_of(plane, d1, d2, h):
        if h == 0:
            xx, yy = (x + d1) % 4, (y + d2) % 4
        else:
            xx, yy = (x + d2) % 4, (y + d1) % 4
        return 2 * (plane * 16 + yy * 4 + xx) + h

    def ag_copy(k, b, device, part=None):
        ref = panel[k].at[b]
        if part is not None:
            ref = panel[k].at[b, pl.ds(part * half_chunk, half_chunk)]
        remote(ref, ref, ag_send.at[k], ag_recv.at[k, b], device).start()

    def ag_wait(k, b):
        wait_recv(panel[k].at[b], ag_send.at[k], ag_recv.at[k, b])

    def first_dim(h):
        return 0 if h == 0 else 1

    def second_dim(h):
        return 1 if h == 0 else 0

    def s0(k, plane):
        for dim in (first_dim, second_dim):
            for h in (0, 1):
                b = block_of(plane, 0, 0, h)
                for d in (1, -1):
                    ag_copy(k, b, neighbour(dim(h), d))

    def s1(k, plane):
        for d in (-1, 1):
            for h in (0, 1):
                b = block_of(plane, d, 0, h)
                ag_wait(k, b)
                ag_copy(k, b, neighbour(first_dim(h), -d), 0 if d == -1 else 1)
                for e in (1, -1):
                    ag_copy(k, b, neighbour(second_dim(h), e))

    def s2(k, plane):
        for h in (0, 1):
            b = block_of(plane, 2, 0, h)
            ag_wait(k, b)
            for e in (1, -1):
                ag_copy(k, b, neighbour(second_dim(h), e))

    def s3(k, plane):
        for d1 in (0, -1, 1, 2):
            for d in (-1, 1):
                for h in (0, 1):
                    b = block_of(plane, d1, d, h)
                    ag_wait(k, b)
                    ag_copy(k, b, neighbour(second_dim(h), -d), 0 if d == -1 else 1)

    def s4(k, plane):
        for d1 in (0, -1, 1, 2):
            for h in (0, 1):
                ag_wait(k, block_of(plane, d1, 2, h))

    def z_go(k):
        for h in (0, 1):
            b = block_of(zh, 0, 0, h)
            ag_copy(k, b, z_partner)

    def z_come(k):
        for h in (0, 1):
            ag_wait(k, block_of(1 - zh, 0, 0, h))
        s0(k, 1 - zh)

    def prepare(k):
        lanes = pl.ds(k * chunk, chunk)
        kept = jnp.where(
            pre[:, lanes].astype(jnp.float32) > 0, cot[:, lanes].astype(jnp.float32), 0.0
        )
        for h in (0, 1):
            part = kept[h * BLOCK:(h + 1) * BLOCK, :]
            panel[k][2 * c + h] = part.T.astype(jnp.bfloat16)
        return jnp.sum(kept, axis=0, keepdims=True)

    def bias_plane(d, carry):
        remote(bxy.at[m], bxy.at[m], b_send.at[0], b_recv.at[0], plane_peer(d)).start()
        return carry

    def bias_z(d, carry):
        remote(bz.at[w8], bz.at[w8], b_send.at[1], b_recv.at[1], z_peer(d)).start()
        return carry

    bias_rows = [prepare(0)]
    pl.semaphore_wait(barrier, 23)
    s0(0, zh)
    z_go(0)
    for k in range(1, CHUNKS):
        bias_rows.append(prepare(k))
        s0(k, zh)
        z_go(k)
    bias_local = jnp.concatenate(bias_rows, axis=1)
    bxy[m] = jnp.zeros(bxy.shape[1:], jnp.float32)
    for q in range(width // BLOCK):
        bxy[m, pl.ds(q, 1)] = bias_local[:, q * BLOCK:(q + 1) * BLOCK]
    lax.fori_loop(1, 16, bias_plane, 0)
    feat_all[zl] = feat[...].astype(jnp.float32).T.astype(jnp.bfloat16)

    lane = lax.broadcasted_iota(jnp.int32, (n_tiles, n_tiles), 1)
    sub = lax.broadcasted_iota(jnp.int32, (n_tiles, n_tiles), 0)
    live = count[0, 0]
    lane1 = lax.broadcasted_iota(jnp.int32, (1, n_tiles), 1)
    col_r = jnp.where(lane1 < live, tcol[...], 100)
    diag = lane == sub
    col_c = jnp.sum(jnp.where(diag, col_r, 0), axis=1, keepdims=True)
    row_c = jnp.sum(jnp.where(diag, trow[...], 0), axis=1, keepdims=True)
    rank_c = jnp.sum(
        jnp.where((col_r == col_c) & (lane < sub), 1, 0), axis=1, keepdims=True
    )
    lane_j = lax.broadcasted_iota(jnp.int32, (n_tiles, BLOCK), 1)
    n_r = jnp.sum(jnp.where(col_c == lane_j, 1, 0), axis=0, keepdims=True)
    lane_j1 = lax.broadcasted_iota(jnp.int32, (1, BLOCK), 1)
    pad_r = jnp.where(lane_j1 < n_cols, n_r + (n_r & 1), 0)
    base_c = jnp.sum(jnp.where(lane_j < col_c, pad_r, 0), axis=1, keepdims=True)
    pos_c = jnp.where(col_c < n_cols, base_c + rank_c, 100000)
    jj_lane = lax.broadcasted_iota(jnp.int32, (BLOCK, BLOCK), 1)
    jj_sub = lax.broadcasted_iota(jnp.int32, (BLOCK, BLOCK), 0)
    pad_c = jnp.sum(jnp.where(jj_lane == jj_sub, pad_r, 0), axis=1, keepdims=True)
    end_r = jnp.sum(jnp.where(jj_sub <= jj_lane, pad_c, 0), axis=0, keepdims=True)
    last_r = jnp.maximum(end_r // 2 - 1, 0)
    has_r = jnp.where(n_r > 0, 1, 0)
    meta_w = meta_v.shape[1]
    lane_p = lax.broadcasted_iota(jnp.int32, (n_tiles, meta_w), 1)
    sub_p = lax.broadcasted_iota(jnp.int32, (n_tiles, meta_w), 0)
    for i in (0, 1):
        hit = 2 * lane_p + i == pos_c
        meta_v[i:i + 1, :] = n_tiles + jnp.sum(
            jnp.where(hit, sub_p - n_tiles, 0), axis=0, keepdims=True
        )
        meta_v[5 + i:6 + i, :] = jnp.sum(jnp.where(hit, row_c, 0), axis=0, keepdims=True)
        if i == 0:
            meta_v[2:3, :] = 1 - jnp.sum(
                jnp.where(hit & (rank_c == 0), 1, 0), axis=0, keepdims=True
            )
    meta_v[3:4, 0:BLOCK] = last_r
    meta_v[4:5, 0:BLOCK] = has_r

    meta_copy = pltpu.make_async_copy(meta_v, meta_s, local_sem.at[1])
    meta_copy.start()
    vals[n_tiles] = jnp.zeros((BLOCK, BLOCK), jnp.bfloat16)
    meta_copy.wait()

    def products(k, first, last, acc):
        def pair(p, acc):
            lhs = jnp.concatenate(
                [panel[k][meta_s[5, p]], panel[k][meta_s[6, p]]], axis=1
            )
            rhs = jnp.concatenate([vals[meta_s[0, p]], vals[meta_s[1, p]]], axis=0)
            keep = meta_s[2, p].astype(jnp.float32)
            acc = acc * keep + jnp.dot(lhs, rhs, preferred_element_type=jnp.float32)
            slots[p] = acc
            return acc

        return lax.fori_loop(first, last, pair, acc, unroll=8)

    def column(j):
        return slots[meta_s[3, j]] * meta_s[4, j].astype(jnp.float32)

    turn = [(zl + d) % 4 for d in (1, 2, 3, 0)]

    def rs0(k):
        for i, q in enumerate(turn):
            for h in (0, 1):
                lanes = slice(h * BLOCK, (h + 1) * BLOCK)
                send1[k, q, :, lanes] = column(2 * (2 * q + 1 - core) + h).astype(
                    jnp.bfloat16
                )
            remote(
                send1.at[k, q], recv1.at[k, q], rs_send1.at[k, i], rs_recv1.at[k, i], partner
            ).start()
        for q in turn:
            for h in (0, 1):
                lanes = slice(h * BLOCK, (h + 1) * BLOCK)
                own[q, :, lanes] = column(2 * (2 * q + core) + h)

    def rs1(k):
        for i, q in enumerate(turn):
            wait_recv(recv1.at[k, q], rs_send1.at[k, i], rs_recv1.at[k, i])
            pair = own[q] + recv1[k, q].astype(jnp.float32)
            send2[k, q] = pair.astype(jnp.bfloat16)
            if i < 3:
                remote(
                    send2.at[k, q], recv2.at[k, i], rs_send2.at[k, i], rs_recv2.at[k, i],
                    z_near(i + 1),
                ).start()
            else:
                total[k] = pair

    def rs2(k):
        summed = total[k]
        for d in range(3):
            wait_recv(recv2.at[k, d], rs_send2.at[k, d], rs_recv2.at[k, d])
            summed = summed + recv2[k, d].astype(jnp.float32)
        fg = jnp.dot(
            weight[:, k * chunk:(k + 1) * chunk], summed.astype(jnp.bfloat16),
            preferred_element_type=jnp.float32,
        )
        if k == 0:
            fg_acc[...] = fg
        else:
            fg_out[...] = (fg_acc[...] + fg).T.astype(jnp.bfloat16)

    def term(k, which):
        rows = pl.ds(which * half, half)
        acc = None
        for q in turn:
            piece = lax.dot_general(
                feat_all[q, rows, :], send2[k, q], (((1,), (1,)), ((), ())),
                preferred_element_type=jnp.float32,
            )
            acc = piece if acc is None else acc + piece
        return acc.reshape(recv_p.shape[1:])

    def ar0(k):
        ar[k] = term(k, 1 - core)
        remote(ar.at[k], recv_p.at[k], ar_send.at[k, 0], ar_recv.at[k, 0], partner).start()
        xs[k] = term(k, core)

    def ar1(k):
        wait_recv(recv_p.at[k], ar_send.at[k, 0], ar_recv.at[k, 0])
        xs[k] = xs[k] + recv_p[k]

        def go(d, carry):
            remote(
                xs.at[k, (m + d) % 16], recv_xy.at[k, d - 1],
                ar_send.at[k, 1], ar_recv.at[k, 1], plane_peer(d),
            ).start()
            return carry

        lax.fori_loop(1, 16, go, 0)

    def ar2(k):
        wait_recv(recv_xy.at[k], ar_send.at[k, 1], ar_recv.at[k, 1])
        zbuf[k, w8] = (xs[k, m] + jnp.sum(recv_xy[k], axis=0)).astype(zbuf.dtype)

        def go(d, carry):
            ref = zbuf.at[k, w8]
            remote(ref, ref, ar_send.at[k, 2], ar_recv.at[k, 2], z_peer(d)).start()
            return carry

        lax.fori_loop(1, 8, go, 0)

    def ar3(k):
        wait_recv(zbuf.at[k, pl.ds(0, 7)], ar_send.at[k, 2], ar_recv.at[k, 2])
        grad = zbuf[k, 0].astype(jnp.float32)
        for i in range(1, 8):
            grad = grad + zbuf[k, i].astype(jnp.float32)
        gathered[k, core, m] = grad * norm_scale

        def go(d, carry):
            ref = gathered.at[k, core, m]
            remote(ref, ref, ar_send.at[k, 3], ar_recv.at[k, 3], plane_peer(d)).start()
            return carry

        lax.fori_loop(1, 16, go, 0)

    def ar4(k):
        wait_recv(gathered.at[k, 0, pl.ds(0, 15)], ar_send.at[k, 3], ar_recv.at[k, 3])
        ref = gathered.at[k, core]
        remote(ref, ref, ar_send.at[k, 4], ar_recv.at[k, 4], partner).start()

    def bias1():
        wait_recv(bxy.at[pl.ds(0, 15)], b_send.at[0], b_recv.at[0])
        plane_sum = bxy[0]
        for i in range(1, 16):
            plane_sum = plane_sum + bxy[i]
        bz[w8] = plane_sum
        lax.fori_loop(1, 8, bias_z, 0)

    def bias2():
        wait_recv(bz.at[pl.ds(0, 7)], b_send.at[1], b_recv.at[1])
        z_sum = bz[0]
        for i in range(1, 8):
            z_sum = z_sum + bz[i]
        bp[0] = z_sum
        remote(bp.at[0], bp.at[1], b_send.at[2], b_recv.at[2], partner).start()

    other = 1 - zh
    cuts = [n_pairs * i // 32 * 8 for i in range(4)] + [n_pairs]
    s1(0, zh)
    s2(0, zh)
    z_come(0)
    s3(0, zh)
    s1(0, other)
    s2(0, other)
    s1(1, zh)
    s2(1, zh)
    z_come(1)
    for d in (1, 2, 3):
        remote(
            feat_all.at[zl], feat_all.at[zl], f_send.at[0], f_recv.at[0], z_near(d)
        ).start()
    s3(0, other)
    s4(0, zh)
    s4(0, other)
    tiles_copy.wait()
    acc = jnp.zeros((chunk, BLOCK), jnp.float32)
    acc = products(0, cuts[0], cuts[2], acc)
    s3(1, zh)
    acc = products(0, cuts[2], cuts[3], acc)
    s1(1, other)
    s2(1, other)
    products(0, cuts[3], cuts[4], acc)
    rs0(0)
    s3(1, other)
    wait_recv(feat_all.at[pl.ds(0, 3)], f_send.at[0], f_recv.at[0])
    rs1(0)
    ar0(0)
    s4(1, zh)
    s4(1, other)
    ar1(0)
    acc = jnp.zeros((chunk, BLOCK), jnp.float32)
    acc = products(1, cuts[0], cuts[2], acc)
    bias1()
    ar2(0)
    products(1, cuts[2], cuts[4], acc)
    rs0(1)
    ar3(0)
    bias2()
    rs1(1)
    ar0(1)
    rs2(0)
    ar1(1)
    ar4(0)
    ar2(1)
    wait_recv(bp.at[1], b_send.at[2], b_recv.at[2])
    bias_out[...] = (bp[0] + bp[1]) * norm_scale
    ar3(1)
    rs2(1)
    ar4(1)

    for k in range(CHUNKS):
        wait_send(panel[k].at[pl.ds(0, 62)], ag_send.at[k], ag_recv.at[k, 0])
        for i in range(4):
            wait_send(send1.at[k, 0], rs_send1.at[k, i], rs_recv1.at[k, i])
        for d in range(3):
            wait_send(recv2.at[k, d], rs_send2.at[k, d], rs_recv2.at[k, d])
        wait_send(ar.at[k], ar_send.at[k, 0], ar_recv.at[k, 0])
        wait_send(recv_xy.at[k], ar_send.at[k, 1], ar_recv.at[k, 1])
        wait_send(zbuf.at[k, pl.ds(0, 7)], ar_send.at[k, 2], ar_recv.at[k, 2])
        wait_send(gathered.at[k, 0, pl.ds(0, 15)], ar_send.at[k, 3], ar_recv.at[k, 3])
    wait_send(feat_all.at[pl.ds(0, 3)], f_send.at[0], f_recv.at[0])
    wait_send(bxy.at[pl.ds(0, 15)], b_send.at[0], b_recv.at[0])
    wait_send(bz.at[pl.ds(0, 7)], b_send.at[1], b_recv.at[1])
    wait_send(bp.at[0], b_send.at[2], b_recv.at[2])
    for k in range(CHUNKS):
        wait_recv(gathered.at[k, 0], ar_send.at[k, 4], ar_recv.at[k, 4])
        wait_send(gathered.at[k, 0], ar_send.at[k, 4], ar_recv.at[k, 4])


def finish_body(fg, wg, bias, fg_out, wg_out, bias_out):
    chunk = wg.shape[2]
    fg_out[...] = fg[...]
    for k in range(CHUNKS):
        wg_out[:, k * chunk:(k + 1) * chunk] = wg[k]
    for q in range(bias_out.shape[0] // BLOCK):
        bias_out[pl.ds(q * BLOCK, BLOCK)] = bias[q]


def local(features, pre_act, out_grad, weight, tile_rows, tile_cols, tile_vals, tile_counts):
    rows_dev, width = features.shape
    slots = tile_rows.shape[2]
    chunk = width // CHUNKS
    n_pairs = (slots + 16) // 2
    piece = (width // 32, chunk)
    vertices = rows_dev * lax.axis_size("row") * lax.axis_size("col")
    bf16, f32 = jnp.bfloat16, jnp.float32
    shape = jax.ShapeDtypeStruct
    vmem = pl.BlockSpec(memory_space=pltpu.VMEM)
    smem = pl.BlockSpec(memory_space=pltpu.SMEM)
    anywhere = pl.BlockSpec(memory_space=pl.ANY)
    dma = pltpu.SemaphoreType.DMA
    fg, wg, bias = pl.pallas_call(
        functools.partial(body, 1.0 / math.sqrt(vertices)),
        out_shape=(
            shape((rows_dev, width), bf16),
            shape((CHUNKS, 2, 16) + piece, f32),
            shape((8, BLOCK), f32),
        ),
        in_specs=[vmem] * 6 + [smem, anywhere],
        out_specs=(vmem, vmem, vmem),
        scratch_shapes=[
            pltpu.VMEM((64, chunk, BLOCK), bf16),
            pltpu.VMEM((64, chunk, BLOCK), bf16),
            pltpu.VMEM((slots + 1, BLOCK, BLOCK), bf16),
            pltpu.VMEM((n_pairs, chunk, BLOCK), f32),
            pltpu.VMEM((4, width, rows_dev), bf16),
            pltpu.VMEM((4, chunk, rows_dev), f32),
            pltpu.VMEM((CHUNKS, 4, chunk, rows_dev), bf16),
            pltpu.VMEM((CHUNKS, 4, chunk, rows_dev), bf16),
            pltpu.VMEM((CHUNKS, chunk, rows_dev), f32),
            pltpu.VMEM((CHUNKS, 4, chunk, rows_dev), bf16),
            pltpu.VMEM((CHUNKS, 3, chunk, rows_dev), bf16),
            pltpu.VMEM((width, rows_dev), f32),
            pltpu.VMEM((CHUNKS, 16) + piece, f32),
            pltpu.VMEM((CHUNKS, 16) + piece, f32),
            pltpu.VMEM((CHUNKS, 16) + piece, f32),
            pltpu.VMEM((CHUNKS, 15) + piece, f32),
            pltpu.VMEM((CHUNKS, 8) + piece, bf16),
            pltpu.VMEM((16, 8, BLOCK), f32),
            pltpu.VMEM((8, 8, BLOCK), f32),
            pltpu.VMEM((2, 8, BLOCK), f32),
            pltpu.VMEM((8, 256), jnp.int32),
            pltpu.SMEM((8, 256), jnp.int32),
            dma((2,)), dma((CHUNKS,)), dma((CHUNKS, 64)), dma((1,)), dma((1,)),
            dma((CHUNKS, 4)), dma((CHUNKS, 4)), dma((CHUNKS, 3)), dma((CHUNKS, 3)),
            dma((CHUNKS, 5)), dma((CHUNKS, 5)), dma((3,)), dma((3,)),
        ],
        compiler_params=pltpu.CompilerParams(
            collective_id=0, has_side_effects=True, vmem_limit_bytes=58 * 1024 * 1024
        ),
    )(
        pre_act, out_grad, features, weight,
        tile_rows.reshape(1, slots), tile_cols.reshape(1, slots), tile_counts.reshape(1, 1),
        tile_vals.reshape(slots, BLOCK, BLOCK),
    )
    return pl.pallas_call(
        finish_body,
        out_shape=(shape((rows_dev, width), bf16), shape((width, width), f32), shape((width,), f32)),
        in_specs=[vmem] * 3,
        out_specs=(vmem, vmem, vmem),
    )(fg, wg.reshape(CHUNKS, width, chunk), bias)


def solution(mesh):
    placed = (
        P(("row", "col"), None),
        P(("row", "col"), None),
        P(("row", "col"), None),
        P(),
        P("row", "col", None),
        P("row", "col", None),
        P("row", "col", None, None, None),
        P("row", "col"),
    )
    return jax.shard_map(
        local,
        mesh=mesh,
        in_specs=placed,
        out_specs=(P(("row", "col"), None), P(), P()),
        check_vma=False,
    )
```

time: 730 us -> 109 us (0.15)
  waiting for transfers between devices: 373 us -> 0 us
  other arithmetic: 151 us -> 0 us
  Pallas kernels: 0 us -> 107 us
  blocking collectives: 80.3 us -> 0 us
  local copies, waits for them, and re-layouts: 53.9 us -> 0 us
  matrix products: 53.3 us -> 0 us
  between operations: 13.8 us -> 1.29 us
    psum x1 -> x0, waiting for transfers between devices: 176 us -> none  [local(): lax.psum((local_weight, local_bias), ('row', 'col'))]
    all_gather x1 -> x0, waiting for transfers between devices: 145 us -> none  [local(): grad_panel = lax.all_gather(masked, 'col', axis=0, tiled=True)]
    scatter-add x4 -> x0, other arithmetic: 145 us -> none  [add_tiles(): jax.ops.segment_sum(products, cols_now, num_segments=col_blocks)]
    pallas_call x0 -> x2, Pallas kernels: none -> 107 us  [the longest x1 105 us: local(): pl.pallas_call(functools.partial(body, 1.0 / math.sqrt(vertices)), out_sh...]
    psum x1 -> x0, blocking collectives: 80.3 us -> none  [local(): lax.psum((local_weight, local_bias), ('row', 'col'))]
    dot_general x6 -> x0, matrix products: 53.3 us -> none  [the longest x4 48.6 us: add_tiles(): jnp.einsum('kab,kaf->kbf', vals_now, gathered, preferred_element_type=jnp...]
    reduce_scatter x1 -> x0, waiting for transfers between devices: 51.8 us -> none  [local(): lax.psum_scatter(partial_sum, 'row', scatter_dimension=0, tiled=True)]
    gather x4 -> x0, local copies, waits for them, and re-layouts: 35.6 us -> none  [add_tiles(): gathered = jnp.take(grad_blocks, rows_now, axis=0)]
  transfers between devices with their start and end apart: 3 -> 0, of which waited for: 3 -> 0; matrix products, arithmetic and copies ran while one was open for 2% -> 0% of each run, Pallas kernels for 0% -> 0%
where the time goes in v3:
time: 109 us
  Pallas kernels  107 us (98%)
  between operations  1.29 us (1%)
    pallas_call x1, Pallas kernels, local(): pl.pallas_call(functools.partial(body, 1.0 / math.sqrt(vertices)), out_sh...  105 us
    pallas_call x1, Pallas kernels, local(): pl.pallas_call(finish_body, out_shape=(shape((rows_dev, width), bf16), sh...  2.4 us

profile of v3, /device:TPU:1, one launch (start us, length us, event | category | flops | bytes accessed | tf_op | source)
XLA Modules:
  0.0 108.6 jit_solution(17553533796152122318)
XLA Ops:
  1.3 104.9 %shard_map.103 = (bf16[256,512]{1,0:T(8,128)(2,1)}, f32[2,2,16,16,256]{4,3,2,1,0:T(8,128)}, f32[8,128]{1,0:T(8,128)}) custom-call(bf16[256,512]{1,0:T(8,128)(2,1)} %pre.1, bf16[256,512]{1,0:T(8,128)(2,1)} %cot.1, bf16[256,512]{1,0:T(8,128)(2,1)} %feat.1, bf16[512,512]{1,0:T(8,128)(2,1)} %weight.1, s32[1,256]{1,0:T(1,128)} %bitcast.6, s32[1,256]{1,0:T(1,128)} %bitcast.7, ...), custom_call_target="tpu_custom_call" | custom-call | tf_op jit(solution)/shard_map/pallas_call | solution.py:467
  106.2 2.4 %shard_map.104 = (bf16[256,512]{1,0:T(8,128)(2,1)}, f32[512,512]{1,0:T(8,128)}, f32[512]{0:T(512)}) custom-call(bf16[256,512]{1,0:T(8,128)(2,1)} %get-tuple-element.6.fg, f32[2,512,256]{2,1,0:T(8,128)} %bitcast.5, f32[8,128]{1,0:T(8,128)} %get-tuple-element.8.bias), custom_call_target="tpu_custom_call" | custom-call | tf_op jit(solution)/shard_map/pallas_call | solution.py:511

commit v4 on v3

--- a/solution.py
+++ b/solution.py
@@ -18,7 +18,7 @@
     pre, cot, feat, weight, trow, tcol, count, vals_hbm,
     fg_out, gathered, bias_out,
     panel0, panel1, vals, slots, feat_all, own, send1, recv1, total, send2, recv2, fg_acc,
-    ar, recv_p, xs, recv_xy, zbuf, bxy, bz, bp, meta_v, meta_s,
+    ar, recv_p, mine, xs, recv_xy, zbuf, bxy, bz, bp, meta_v, meta_s,
     local_sem, ag_send, ag_recv, f_send, f_recv, rs_send1, rs_recv1, rs_send2, rs_recv2,
     ar_send, ar_recv, b_send, b_recv,
 ):
@@ -306,13 +306,13 @@
         return acc.reshape(recv_p.shape[1:])
 
     def ar0(k):
-        ar[k] = term(k, 1 - core)
+        ar[k] = term(k, 1 - core).astype(ar.dtype)
         remote(ar.at[k], recv_p.at[k], ar_send.at[k, 0], ar_recv.at[k, 0], partner).start()
-        xs[k] = term(k, core)
+        mine[k] = term(k, core)
 
     def ar1(k):
         wait_recv(recv_p.at[k], ar_send.at[k, 0], ar_recv.at[k, 0])
-        xs[k] = xs[k] + recv_p[k]
+        xs[k] = (mine[k] + recv_p[k].astype(jnp.float32)).astype(xs.dtype)
 
         def go(d, carry):
             remote(
@@ -325,7 +325,10 @@
 
     def ar2(k):
         wait_recv(recv_xy.at[k], ar_send.at[k, 1], ar_recv.at[k, 1])
-        zbuf[k, w8] = (xs[k, m] + jnp.sum(recv_xy[k], axis=0)).astype(zbuf.dtype)
+        plane_sum = xs[k, m].astype(jnp.float32)
+        for i in range(15):
+            plane_sum = plane_sum + recv_xy[k, i].astype(jnp.float32)
+        zbuf[k, w8] = plane_sum.astype(zbuf.dtype)
 
         def go(d, carry):
             ref = zbuf.at[k, w8]
@@ -339,7 +342,7 @@
         grad = zbuf[k, 0].astype(jnp.float32)
         for i in range(1, 8):
             grad = grad + zbuf[k, i].astype(jnp.float32)
-        gathered[k, core, m] = grad * norm_scale
+        gathered[k, core, m] = (grad * norm_scale).astype(gathered.dtype)
 
         def go(d, carry):
             ref = gathered.at[k, core, m]
@@ -402,25 +405,24 @@
     ar0(0)
     s4(1, zh)
     s4(1, other)
+    acc = jnp.zeros((chunk, BLOCK), jnp.float32)
+    products(1, cuts[0], cuts[4], acc)
+    rs0(1)
     ar1(0)
-    acc = jnp.zeros((chunk, BLOCK), jnp.float32)
-    acc = products(1, cuts[0], cuts[2], acc)
     bias1()
-    ar2(0)
-    products(1, cuts[2], cuts[4], acc)
-    rs0(1)
-    ar3(0)
-    bias2()
     rs1(1)
     ar0(1)
     rs2(0)
     ar1(1)
-    ar4(0)
+    bias2()
+    ar2(0)
     ar2(1)
     wait_recv(bp.at[1], b_send.at[2], b_recv.at[2])
     bias_out[...] = (bp[0] + bp[1]) * norm_scale
+    ar3(0)
     ar3(1)
     rs2(1)
+    ar4(0)
     ar4(1)
 
     for k in range(CHUNKS):
@@ -446,7 +448,7 @@
     chunk = wg.shape[2]
     fg_out[...] = fg[...]
     for k in range(CHUNKS):
-        wg_out[:, k * chunk:(k + 1) * chunk] = wg[k]
+        wg_out[:, k * chunk:(k + 1) * chunk] = wg[k].astype(jnp.float32)
     for q in range(bias_out.shape[0] // BLOCK):
         bias_out[pl.ds(q * BLOCK, BLOCK)] = bias[q]
 
@@ -468,7 +470,7 @@
         functools.partial(body, 1.0 / math.sqrt(vertices)),
         out_shape=(
             shape((rows_dev, width), bf16),
-            shape((CHUNKS, 2, 16) + piece, f32),
+            shape((CHUNKS, 2, 16) + piece, bf16),
             shape((8, BLOCK), f32),
         ),
         in_specs=[vmem] * 6 + [smem, anywhere],
@@ -486,10 +488,11 @@
             pltpu.VMEM((CHUNKS, 4, chunk, rows_dev), bf16),
             pltpu.VMEM((CHUNKS, 3, chunk, rows_dev), bf16),
             pltpu.VMEM((width, rows_dev), f32),
+            pltpu.VMEM((CHUNKS, 16) + piece, bf16),
+            pltpu.VMEM((CHUNKS, 16) + piece, bf16),
             pltpu.VMEM((CHUNKS, 16) + piece, f32),
-            pltpu.VMEM((CHUNKS, 16) + piece, f32),
-            pltpu.VMEM((CHUNKS, 16) + piece, f32),
-            pltpu.VMEM((CHUNKS, 15) + piece, f32),
+            pltpu.VMEM((CHUNKS, 16) + piece, bf16),
+            pltpu.VMEM((CHUNKS, 15) + piece, bf16),
             pltpu.VMEM((CHUNKS, 8) + piece, bf16),
             pltpu.VMEM((16, 8, BLOCK), f32),
             pltpu.VMEM((8, 8, BLOCK), f32),

time: 109 us -> 106 us (0.972)
  Pallas kernels: 107 us -> 105 us
    pallas_call x1, Pallas kernels: 105 us -> 102 us  [local(): pl.pallas_call(functools.partial(body, 1.0 / math.sqrt(vertices)), out_sh...]
where the time goes in v4:
time: 106 us
  Pallas kernels  105 us (99%)
  between operations  1.29 us (1%)
    pallas_call x1, Pallas kernels, local(): pl.pallas_call(functools.partial(body, 1.0 / math.sqrt(vertices)), out_sh...  102 us
    pallas_call x1, Pallas kernels, local(): pl.pallas_call(finish_body, out_shape=(shape((rows_dev, width), bf16), sh...  2.26 us

profile of v4, /device:TPU:1, one launch (start us, length us, event | category | flops | bytes accessed | tf_op | source)
XLA Modules:
  0.0 106.0 jit_solution(12408345235740820909)
XLA Ops:
  1.3 102.4 %shard_map.103 = (bf16[256,512]{1,0:T(8,128)(2,1)}, bf16[2,2,16,16,256]{4,3,2,1,0:T(8,128)(2,1)}, f32[8,128]{1,0:T(8,128)}) custom-call(bf16[256,512]{1,0:T(8,128)(2,1)} %pre.1, bf16[256,512]{1,0:T(8,128)(2,1)} %cot.1, bf16[256,512]{1,0:T(8,128)(2,1)} %feat.1, bf16[512,512]{1,0:T(8,128)(2,1)} %weight.1, s32[1,256]{1,0:T(1,128)} %bitcast.6, ...), custom_call_target="tpu_custom_call" | custom-call | tf_op jit(solution)/shard_map/pallas_call | solution.py:469
  103.7 2.3 %shard_map.104 = (bf16[256,512]{1,0:T(8,128)(2,1)}, f32[512,512]{1,0:T(8,128)}, f32[512]{0:T(512)}) custom-call(bf16[256,512]{1,0:T(8,128)(2,1)} %get-tuple-element.6.fg, bf16[2,512,256]{2,1,0:T(8,128)(2,1)} %bitcast.5, f32[8,128]{1,0:T(8,128)} %get-tuple-element.8.bias), custom_call_target="tpu_custom_call" | custom-call | tf_op jit(solution)/shard_map/pallas_call | solution.py:514
